TPU v7x, 512 devices: a whole 4x8x8 slice. The times are simulated.
512 devices in a mesh: tensor: 8 (over z), expert: 64 (over y, x, core).
Axes of the slice: x: 4, y: 8, z: 8, core: 2. Of those that a mesh axis runs over, the one named last changes fastest.
Arguments:
- out_grad: bfloat16 [64, 32, 4096], P('expert', 'tensor'), may hold values from -6 to 6
- norm_input: bfloat16 [64, 32, 4096], P('expert', 'tensor'), may hold values from -24 to 24
- norm_gain: float32 [4096], replicated, may hold values from 0.3 to 3
- routes: int32 [64, 32, 8], P('expert'), may hold values from 0 to 63, all different within a row; in each aligned block of 32 rows (0 to 31, 32 to 63, ..., all dimensions but the last counted through in order) at most 8 rows name the same one
- route_weight: float32 [64, 32, 8], P('expert'), may hold values from 0.05 to 0.25
- gate_saved: bfloat16 [64, 512, 1024], P('expert', None, 'tensor'), may hold values from -8 to 8
- up_saved: bfloat16 [64, 512, 1024], P('expert', None, 'tensor'), may hold values from -6 to 6
- w_gate: bfloat16 [64, 4096, 1024], P('expert', None, 'tensor'), may hold values from -0.09375 to 0.09375
- w_up: bfloat16 [64, 4096, 1024], P('expert', None, 'tensor'), may hold values from -0.09375 to 0.09375
- w_down: bfloat16 [64, 1024, 4096], P('expert', 'tensor'), may hold values from -0.1875 to 0.1875
- out_proj: bfloat16 [4096, 4096], P('tensor', 'expert'), may hold values from -0.09375 to 0.09375
Outputs:
- resid_grad: bfloat16 [64, 32, 4096], P('expert', 'tensor')
- attn_grad: bfloat16 [64, 32, 4096], P('expert', None, 'tensor')
- down_grad: bfloat16 [64, 1024, 4096], P('expert', 'tensor')
Inputs may be any that keep to these rules, and one draw needn't show every extreme that they name: Each token names 8 different experts. Among the tokens of one group no expert is named by more than 8 routes, and in some group some expert is named by exactly 8.
All inputs are finite; a program needn't handle non-finite values.
Results may differ from a plain program's by a relative error of at most 0.015.
Values may be sent and summed in bfloat16 or wider, within the bound.
No kernel may reach another device: no remote copies, remote signals or barrier semaphores. Data moves between devices by JAX's collectives and lax.ppermute only.
A program may use at most 64 MiB of HBM per device.

v0:
```python
import jax
import jax.numpy as jnp
from jax import lax
from jax.sharding import PartitionSpec as P


def slot_position(route_ids, slot_cap, expert_count):
    flat_ids = route_ids.reshape(-1)
    one_hot = (flat_ids[:, None] == jnp.arange(expert_count, dtype=jnp.int32)[None, :]).astype(
        jnp.int32
    )
    earlier = jnp.cumsum(one_hot, axis=0) - one_hot
    slot_rank = jnp.sum(earlier * one_hot, axis=1)
    return flat_ids * slot_cap + slot_rank


def weighted_rows(token_rows, slot_token, slot_weight):
    picked_rows = token_rows[slot_token]
    return (slot_weight[:, None] * picked_rows.astype(jnp.float32)).astype(jnp.bfloat16)


def per_device(
    out_grad,
    norm_input,
    norm_gain,
    routes,
    route_weight,
    gate_saved,
    up_saved,
    w_gate,
    w_up,
    w_down,
    out_proj,
):
    expert_count = lax.axis_size("expert")
    slot_cap = gate_saved.shape[1] // expert_count
    top_count = routes.shape[2]
    route_total = routes.shape[1] * top_count
    model_width = out_grad.shape[2]
    position = slot_position(routes[0], slot_cap, expert_count)
    source = (
        jnp.full((expert_count * slot_cap,), -1, jnp.int32)
        .at[position]
        .set(jnp.arange(route_total, dtype=jnp.int32))
    )
    filled = source >= 0
    safe_source = jnp.where(filled, source, 0)
    slot_weight = jnp.where(filled, route_weight[0].reshape(-1)[safe_source], jnp.float32(0.0))
    slot_token = safe_source // top_count
    group_grads = lax.all_gather(out_grad, "tensor", axis=1, tiled=True)
    scaled = weighted_rows(group_grads[0], slot_token, slot_weight)
    received = lax.all_to_all(
        scaled.reshape(expert_count, slot_cap, model_width),
        "expert",
        split_axis=0,
        concat_axis=0,
        tiled=True,
    )
    slot_grad = received.reshape(expert_count * slot_cap, model_width)
    contract_last = (((1,), (1,)), ((), ()))
    hid_grad = lax.dot_general(
        slot_grad, w_down[0], contract_last, preferred_element_type=jnp.float32
    )
    gate = gate_saved[0].astype(jnp.float32)
    upper = up_saved[0].astype(jnp.float32)
    sigmoid_gate = jax.nn.sigmoid(gate)
    activation = gate * sigmoid_gate
    gate_grad = (hid_grad * upper * sigmoid_gate * (1.0 + gate * (1.0 - sigmoid_gate))).astype(
        jnp.bfloat16
    )
    up_grad = (hid_grad * activation).astype(jnp.bfloat16)
    part_grad = lax.dot_general(
        gate_grad, w_gate[0], contract_last, preferred_element_type=jnp.float32
    )
    part_grad = part_grad + lax.dot_general(
        up_grad, w_up[0], contract_last, preferred_element_type=jnp.float32
    )
    part_grad = part_grad.astype(jnp.bfloat16)
    hidden = (activation * upper).astype(jnp.bfloat16)
    contract_first = (((0,), (0,)), ((), ()))
    returned = lax.all_to_all(
        part_grad.reshape(expert_count, slot_cap, model_width),
        "expert",
        split_axis=0,
        concat_axis=0,
        tiled=True,
    )
    down_grad = lax.dot_general(
        hidden, slot_grad, contract_first, preferred_element_type=jnp.float32
    )
    down_grad = down_grad.astype(jnp.bfloat16)[None]
    routed = returned.reshape(expert_count * slot_cap, model_width)[position]
    route_sum = jnp.sum(routed.reshape(-1, top_count, model_width).astype(jnp.float32), axis=1)
    moe_grad = lax.psum_scatter(
        route_sum.astype(jnp.bfloat16), "tensor", scatter_dimension=0, tiled=True
    ).astype(jnp.float32)
    resid_in = norm_input[0].astype(jnp.float32)
    inv_rms = lax.rsqrt(jnp.mean(resid_in * resid_in, axis=-1, keepdims=True) + 1e-06)
    scaled_grad = norm_gain * moe_grad
    projection = jnp.sum(scaled_grad * resid_in, axis=-1, keepdims=True)
    resid_grad = (
        out_grad[0].astype(jnp.float32)
        + inv_rms * scaled_grad
        - inv_rms * inv_rms * inv_rms / model_width * resid_in * projection
    )
    resid_grad = resid_grad.astype(jnp.bfloat16)[None]
    group_resid = lax.all_gather(resid_grad, "tensor", axis=1, tiled=True)
    group_rows = group_resid[0]
    attn_sum = lax.dot_general(
        group_rows,
        lax.all_gather(out_proj, "expert", axis=1, tiled=True),
        contract_last,
        preferred_element_type=jnp.float32,
    )
    attn_grad = attn_sum.astype(jnp.bfloat16)[None]
    return (resid_grad, attn_grad, down_grad)


def solution(mesh):
    placed = (
        P("expert", "tensor", None),
        P("expert", "tensor", None),
        P(),
        P("expert", None, None),
        P("expert", None, None),
        P("expert", None, "tensor"),
        P("expert", None, "tensor"),
        P("expert", None, "tensor"),
        P("expert", None, "tensor"),
        P("expert", "tensor", None),
        P("tensor", "expert"),
    )
    return jax.shard_map(
        per_device,
        mesh=mesh,
        in_specs=placed,
        out_specs=(
            P("expert", "tensor", None),
            P("expert", None, "tensor"),
            P("expert", "tensor", None),
        ),
        check_vma=False,
    )
```

profile of v0, /device:TPU:6, one launch (start us, length us, event | category | flops | bytes accessed | tf_op | source)
XLA Modules:
  0.0 393.0 jit_solution(8998679630255523144)
XLA Ops:
  8.0 0.0 copy-start
  8.0 0.9 copy.26
  8.9 0.1 eq.29
  9.0 0.1 eq.25
  9.0 0.7 broadcast_multiply_fusion
  9.7 0.6 reduce-window.6
  10.4 0.2 slice_reduce_fusion
  10.6 0.1 copy.25
  10.7 0.1 mul.114
  10.8 0.1 fusion.41
  10.9 1.4 scatter_custom_fusion
  12.3 0.8 copy.29
  13.1 0.1 reshape_squeeze.4
  13.2 3.5 gather_fusion
  16.7 0.1 mul.116
  16.8 0.8 copy.30
  17.6 31.6 %all_gather.9 = bf16[1,32,4096]{2,0,1:T(2,128)(2,1)S(1)} all-gather(bf16[1,4,4096]{2,0,1:T(2,128)(2,1)S(1)} %copy.30), channel_id=1, replica_groups=mesh['tensor'=8,'expert'=64] {'tensor'}, dimensions={1}, use_global_device_ids=true | all-gather | bytes 294912 | tf_op jit(solution)/shard_map/all_gather | solution.py:50
  49.3 0.3 copy.35
  49.6 4.4 %gather_fusion.1 = bf16[512,4096]{1,0:T(8,128)(2,1)} fusion(bf16[32,4096]{1,0:T(8,128)(2,1)S(1)} %bitcast.109, s32[1024]{0:T(1024)S(1)} %pad_clamp_fusion.1), kind=kCustom, calls=%fused_computation.1 | custom fusion | bytes 8390656 | tf_op jit(solution)/shard_map/gather | solution.py:18
  53.9 3.7 fusion
  57.6 0.0 copy-start.3
  57.6 106.8 %all_to_all.10 = bf16[64,8,4096]{2,1,0:T(8,128)(2,1)S(1)} all-to-all(bf16[64,8,4096]{2,1,0:T(8,128)(2,1)S(1)} %fusion), channel_id=1, replica_groups=mesh['tensor'=8,'expert'=64] {'expert'}, dimensions={0} | all-to-all | bytes 8388608 | tf_op jit(solution)/shard_map/all_to_all | solution.py:52
  164.4 0.0 copy-start.1
  164.4 1.9 copy-done.1
  166.3 0.0 copy-done.3
  166.3 0.0 copy-start.2
  166.3 0.0 copy-start.5
  166.3 1.3 fusion.4
  167.6 0.0 copy-done
  167.6 0.0 copy-done.2
  167.6 0.0 copy-done.5
  167.6 0.0 copy-start.4
  167.6 1.3 fusion.8
  168.9 0.0 copy-done.4
  168.9 3.2 fusion.1
  172.2 5.6 %all-to-all-start.1 = ((bf16[64,8,4096]{2,1,0:T(8,128)(2,1)}), bf16[64,8,4096]{2,1,0:T(8,128)(2,1)}, u32[]{:S(2)}, u32[]{:S(2)}) async-start(bf16[64,8,4096]{2,1,0:T(8,128)(2,1)} %fusion.1), calls=%async_computation.1 | async-start | bytes 8388608 | tf_op jit(solution)/shard_map/all_to_all | solution.py:81
  177.8 0.2 all-reduce.3.cloned.1.call-start
  178.0 96.0 %all-to-all-done.1 = bf16[64,8,4096]{2,1,0:T(8,128)(2,1)} async-done(((bf16[64,8,4096]{2,1,0:T(8,128)(2,1)}), bf16[64,8,4096]{2,1,0:T(8,128)(2,1)}, u32[]{:S(2)}, u32[]{:S(2)}) %all-to-all-start.1) | async-done | bytes 4194336 | tf_op jit(solution)/shard_map/all_to_all | solution.py:81
  274.0 6.6 %gather_fusion.2 = bf16[256,4096]{1,0:T(8,128)(2,1)S(1)} fusion(bf16[512,4096]{1,0:T(8,128)(2,1)} %bitcast.13, s32[1024]{0:T(1024)S(1)} %pad_clamp_fusion), kind=kCustom, calls=%fused_computation.2 | custom fusion | bytes 4195328 | tf_op jit(solution)/shard_map/gather | solution.py:92
  280.6 0.0 copy-start.8
  280.6 0.0 copy-start.9
  280.6 0.0 copy-start.6
  280.6 2.1 bitcast_reduce_fusion
  282.8 0.0 all-reduce.3.cloned.1.call-update
  282.8 0.0 all-gather.4.cloned.1.call-start
  282.8 0.5 all-gather.4.cloned.1.call-update
  283.4 1.3 dynamic-slice
  285.3 3.9 %fusion.2 = bf16[1,128,4096]{2,1,0:T(8,128)(2,1)} fusion(bf16[64,8,4096]{2,1,0:T(8,128)(2,1)} %copy-done.1, bf16[1,512,128]{2,1,0:T(8,128)(2,1)S(1)} %copy-done.5, bf16[1,512,128]{2,1,0:T(8,128)(2,1)S(1)} %copy-done.2), kind=kOutput, calls=%fused_computation.9 | convolution fusion | flops 537919488 | bytes 5505024 | tf_op jit(solution)/shard_map/dot_general | solution.py:88
  289.2 65.7 %all-reduce.3.cloned.1.call-done = bf16[32,4096]{1,0:T(8,128)(2,1)} async-done(((bf16[32,4096]{1,0:T(8,128)(2,1)}), bf16[32,4096]{1,0:T(8,128)(2,1)}) %all-reduce.3.cloned.1.call-update) | async-done | bytes 262160
  355.0 0.0 copy-done.8
  355.0 0.0 copy-done.9
  355.0 1.0 fusion.34
  356.0 0.0 copy-done.6
  356.0 0.9 fusion.43
  357.0 0.0 copy-start.7
  357.0 24.8 %all-gather.1 = bf16[8,4,4096]{2,1,0:T(4,128)(2,1)S(1)} all-gather(bf16[1,4,4096]{2,1,0:T(4,128)(2,1)S(1)} %fusion.43), channel_id=2, replica_groups=mesh['tensor'=8,'expert'=64] {'tensor'}, dimensions={0}, use_global_device_ids=true | all-gather | bytes 294912 | tf_op jit(solution)/shard_map/all_gather | solution.py:107
  381.8 0.1 reshape.147
  381.9 0.0 all-gather.4.cloned.1.call-done
  381.9 3.6 fusion.6
  385.5 0.0 copy-done.7
  (11 shorter events, 0.1 us)
Async XLA Ops:
  8.0 159.6 %copy-start = (bf16[1,4096,128]{2,1,0:T(8,128)(2,1)S(1)}, bf16[1,4096,128]{2,1,0:T(8,128)(2,1)}, u32[]{:S(2)}) copy-start(bf16[1,4096,128]{2,1,0:T(8,128)(2,1)} %param.18) | copy-start | bytes 3145732
  57.6 108.7 %copy-start.3 = (bf16[1,128,4096]{2,1,0:T(8,128)(2,1)S(1)}, bf16[1,128,4096]{2,1,0:T(8,128)(2,1)}, u32[]{:S(2)}) copy-start(bf16[1,128,4096]{2,1,0:T(8,128)(2,1)} %param.20) | copy-start | bytes 3145732
  164.4 1.9 copy-start.1
  166.3 1.3 copy-start.2
  166.3 1.3 copy-start.5
  167.6 1.3 copy-start.4
  172.2 101.8 %all-to-all-start.1 = ((bf16[64,8,4096]{2,1,0:T(8,128)(2,1)}), bf16[64,8,4096]{2,1,0:T(8,128)(2,1)}, u32[]{:S(2)}, u32[]{:S(2)}) async-start(bf16[64,8,4096]{2,1,0:T(8,128)(2,1)} %fusion.1), calls=%async_computation.1 | async-start | bytes 8388608 | tf_op jit(solution)/shard_map/all_to_all | solution.py:81
  177.8 177.2 %all-reduce.3.cloned.1.call-start = ((), (), s32[]{:S(2)}) async-start(), calls=%async_computation.3 | async-start | bytes 524288
  280.6 74.4 %copy-start.8 = (bf16[1,4,4096]{2,1,0:T(4,128)(2,1)S(1)}, bf16[1,4,4096]{2,1,0:T(4,128)(2,1)}, u32[]{:S(2)}) copy-start(bf16[1,4,4096]{2,1,0:T(4,128)(2,1)} %param.12) | copy-start | bytes 98308
  280.6 74.4 %copy-start.9 = (f32[4096]{0:T(1024)S(1)}, f32[4096]{0:T(1024)}, u32[]{:S(2)}) copy-start(f32[4096]{0:T(1024)} %param.13) | copy-start | bytes 49156
  280.6 75.4 %copy-start.6 = (bf16[1,4,4096]{2,1,0:T(4,128)(2,1)S(1)}, bf16[1,4,4096]{2,1,0:T(4,128)(2,1)}, u32[]{:S(2)}) copy-start(bf16[1,4,4096]{2,1,0:T(4,128)(2,1)} %param.11) | copy-start | bytes 98308
  282.8 99.1 %all-gather.4.cloned.1.call-start = ((), (), s32[]{:S(2)}) async-start(), calls=%async_computation.2 | async-start | bytes 4259840 | tf_op jit(solution)/shard_map/all_gather | solution.py:111
  357.0 28.5 %copy-start.7 = (bf16[1,4,4096]{2,1,0:T(4,128)(2,1)}, bf16[1,4,4096]{2,1,0:T(4,128)(2,1)S(1)}, u32[]{:S(2)}) copy-start(bf16[1,4,4096]{2,1,0:T(4,128)(2,1)S(1)} %fusion.43) | copy-start | bytes 98308
Sparse Core Ops, SparseCore 0:
  282.9 72.0 all-reduce.2
Sparse Core Ops, SparseCore 1:
  287.1 76.2 all-gather.3
where the time goes:
time: 394 us; the launch traced here: 393 us
  blocking collectives  163 us (41%)
  waiting for transfers between devices  162 us (41%)
  local copies, waits for them, and re-layouts  22.6 us (6%)
  between operations  16.4 us (4%)
  matrix products  13.3 us (3%)
  other arithmetic  9.32 us (2%)
  starting transfers between devices  5.87 us (1%)
    all_to_all x1, blocking collectives, per_device(): lax.all_to_all(scaled.reshape(expert_count, slot_cap, model_width), 'expe...  107 us
    all_to_all x1, waiting for transfers between devices, per_device(): lax.all_to_all(part_grad.reshape(expert_count, slot_cap, model_width), 'e...  96 us
    unnamed x3, waiting for transfers between devices  66.3 us
    all_gather x1, blocking collectives, per_device(): group_grads = lax.all_gather(out_grad, 'tensor', axis=1, tiled=True)  31.6 us
    all_gather x1, blocking collectives, per_device(): group_resid = lax.all_gather(resid_grad, 'tensor', axis=1, tiled=True)  24.8 us
  transfers between devices with their start and end apart: 3, of which 2 were waited for; matrix products, arithmetic and copies ran while one was open for 2% of the time, Pallas kernels for 0%

commit v1 on v0

v1 whole, which is shorter than its diff:
```python
import functools

import jax
import jax.numpy as jnp
from jax import lax
from jax.experimental import pallas as pl
from jax.experimental.pallas import tpu as pltpu
from jax.sharding import PartitionSpec as P

F32 = jnp.float32
BF16 = jnp.bfloat16
LAST = (((1,), (1,)), ((), ()))
FIRST = (((0,), (0,)), ((), ()))
PLAIN = (((1,), (0,)), ((), ()))
VMEM_BYTES = 48 * 1024 * 1024
OFFSETS = (0, 1, -1, 2, -2, 3, -3, 4)


def dot(a, b, dims):
    return lax.dot_general(a, b, dims, preferred_element_type=F32)


def vmem_specs(count):
    return [pl.BlockSpec(memory_space=pltpu.VMEM)] * count


def call(kernel, out_shapes, args, flops, scratch=()):
    moved = sum(a.size * a.dtype.itemsize for a in (*args, *out_shapes))
    return pl.pallas_call(
        kernel,
        out_shape=list(out_shapes),
        in_specs=vmem_specs(len(args)),
        out_specs=vmem_specs(len(out_shapes)),
        scratch_shapes=list(scratch),
        compiler_params=pltpu.CompilerParams(vmem_limit_bytes=VMEM_BYTES),
        cost_estimate=pl.CostEstimate(flops=flops, bytes_accessed=moved, transcendentals=0),
    )(*args)


def struct(shape, dtype):
    return jax.ShapeDtypeStruct(shape, dtype)


def slice_at(offset, width):
    n = lax.axis_size("tensor")
    index = lax.rem(lax.axis_index("tensor") + (offset + n), n)
    return pl.ds(pl.multiple_of(index * width, width), width)


def hid_kernel(width, *refs):
    chunks = refs[:16]
    w_down, gate_ref, up_ref, w_gate, w_up = refs[16:21]
    gate_grad_ref, up_grad_ref, hidden_ref = refs[21:24]
    far = refs[24:26]
    rows = chunks[0].shape[0]
    for half in range(2):
        total = None
        for k, offset in enumerate(OFFSETS):
            term = dot(chunks[2 * k + half][...], w_down[:, slice_at(offset, width)], LAST)
            total = term if total is None else total + term
        here = pl.ds(half * rows, rows)
        gate = gate_ref[here, :].astype(F32)
        upper = up_ref[here, :].astype(F32)
        sig = jax.nn.sigmoid(gate)
        act = gate * sig
        gate_grad = (total * upper * sig * (1.0 + gate * (1.0 - sig))).astype(BF16)
        up_grad = (total * act).astype(BF16)
        gate_grad_ref[here, :] = gate_grad
        up_grad_ref[here, :] = up_grad
        hidden_ref[here, :] = (act * upper).astype(BF16)
        cols = slice_at(4, width)
        part = dot(gate_grad, w_gate[cols, :], LAST) + dot(up_grad, w_up[cols, :], LAST)
        far[half][...] = part.astype(BF16)


def part_kernel(width, gate_grad, up_grad, w_gate, w_up, *outs):
    rows = outs[0].shape[0]
    for k, offset in enumerate((3, -3, 2, -2, 1, -1, 0)):
        cols = slice_at(offset, width)
        for half in range(2):
            here = pl.ds(half * rows, rows)
            part = dot(gate_grad[here, :], w_gate[cols, :], LAST)
            part = part + dot(up_grad[here, :], w_up[cols, :], LAST)
            outs[2 * k + half][...] = part.astype(BF16)


def down_kernel(width, *refs):
    chunks, hidden, out = refs[:16], refs[16], refs[17]
    rows = chunks[0].shape[0]
    for k, offset in enumerate(OFFSETS):
        total = dot(hidden[pl.ds(0, rows), :], chunks[2 * k][...], FIRST)
        total = total + dot(hidden[pl.ds(rows, rows), :], chunks[2 * k + 1][...], FIRST)
        out[:, slice_at(offset, width)] = total.astype(BF16)


def tail_kernel(moe_ref, rows_ref, norm_ref, gain_ref, proj_ref, resid_ref, attn_ref, held):
    n, _, width = moe_ref.shape
    model = n * width
    norm_in = norm_ref[...].astype(F32)
    inv = lax.rsqrt(jnp.sum(norm_in * norm_in, axis=-1, keepdims=True) / model + 1e-06)
    moe = jnp.concatenate([moe_ref[j] for j in range(n)], axis=1).astype(F32)
    scaled = gain_ref[...] * moe
    along = jnp.sum(scaled * norm_in, axis=-1, keepdims=True)
    resid = rows_ref[...].astype(F32) + inv * scaled - inv * inv * inv / model * norm_in * along
    held[...] = resid
    attn_ref[...] = dot(resid.astype(BF16), proj_ref[...], LAST).astype(BF16)
    own = resid_ref.shape[0]
    index = lax.axis_index("tensor")
    pair = held[pl.ds(pl.multiple_of(index // 2 * 2 * own, 2 * own), 2 * own), :]
    resid_ref[...] = jnp.where(lax.rem(index, 2) == 0, pair[:own], pair[own:]).astype(BF16)


def shift(x, step):
    n = lax.axis_size("tensor")
    return lax.ppermute(x, "tensor", [(i, (i + step) % n) for i in range(n)])


def add(a, b):
    return (a.astype(F32) + b.astype(F32)).astype(BF16)


def per_device(
    out_grad,
    norm_input,
    norm_gain,
    routes,
    route_weight,
    gate_saved,
    up_saved,
    w_gate,
    w_up,
    w_down,
    out_proj,
):
    experts = lax.axis_size("expert")
    n = lax.axis_size("tensor")
    tokens, top = routes.shape[1:]
    slots = gate_saved.shape[1]
    cap = slots // experts
    hid = gate_saved.shape[2]
    model = out_grad.shape[2]
    width = model // n
    total = tokens * top
    half = slots // 2

    ids = routes[0].reshape(total)
    number = jnp.arange(total, dtype=jnp.int32)
    same = (ids[:, None] == ids[None, :]) & (number[None, :] < number[:, None])
    rank = jnp.sum(same.astype(jnp.int32), axis=1)
    position = ids * cap + rank
    named = position[None, :] == jnp.arange(slots, dtype=jnp.int32)[:, None]
    slot_weight = jnp.sum(
        jnp.where(named, route_weight[0].reshape(1, total), 0.0), axis=1, keepdims=True
    )
    of_token = (
        number[:, None] // top == jnp.arange(tokens, dtype=jnp.int32)[None, :]
    ).astype(BF16)
    pick = dot(named.astype(BF16), of_token, PLAIN).astype(BF16)

    own_rows = lax.all_to_all(out_grad[0], "tensor", 1, 0, tiled=True)
    scaled = (slot_weight * dot(pick, own_rows, PLAIN)).astype(BF16)
    own_slots = lax.all_to_all(
        scaled.reshape(experts, cap, width), "expert", 0, 0, tiled=True
    ).reshape(slots, width)

    both = jnp.concatenate([out_grad[0], norm_input[0]], axis=0)
    both, own_slots = lax.optimization_barrier((both, own_slots))
    held = {(0, 0): own_slots[:half], (0, 1): own_slots[half:]}
    for step in range(1, 5):
        held[step, 0] = shift(held[step - 1, 0], 1)
        held[-step, 1] = shift(held[1 - step, 1], -1)
        if step < 4:
            held[step, 1] = shift(held[step - 1, 1], 1)
            held[-step, 0] = shift(held[1 - step, 0], -1)
    chunks = []
    for offset in OFFSETS:
        for which in range(2):
            key = -offset if offset != 4 else (4 if which == 0 else -4)
            chunks.append(held[key, which])

    every = lax.all_to_all(
        jnp.broadcast_to(both[None], (n, *both.shape)), "tensor", 0, 0, tiled=True
    )
    own = out_grad.shape[1]
    all_rows = every[:, :own].reshape(tokens, model)
    all_norm = every[:, own:].reshape(tokens, model)
    proj = lax.all_gather(out_proj, "expert", axis=1, tiled=True)

    half_part = struct((half, width), BF16)
    grads = struct((slots, hid), BF16)
    gate_grad, up_grad, hidden, far_a, far_b = call(
        functools.partial(hid_kernel, width),
        (grads, grads, grads, half_part, half_part),
        (*chunks, w_down[0], gate_saved[0], up_saved[0], w_gate[0], w_up[0]),
        2 * slots * model * hid,
    )
    parts = call(
        functools.partial(part_kernel, width),
        (half_part,) * 14,
        (gate_grad, up_grad, w_gate[0], w_up[0]),
        4 * slots * model * hid,
    )
    part = {(4, 0): far_a, (-4, 1): far_b}
    for k, offset in enumerate((3, -3, 2, -2, 1, -1, 0)):
        part[offset, 0], part[offset, 1] = parts[2 * k], parts[2 * k + 1]
    moving = {
        (1, 0): (4, part[4, 0]),
        (-1, 1): (4, part[-4, 1]),
        (1, 1): (3, part[3, 1]),
        (-1, 0): (3, part[-3, 0]),
    }
    for _ in range(4):
        for (way, which), (away, value) in list(moving.items()):
            if away == 0:
                continue
            value = shift(value, way)
            away -= 1
            if away:
                value = add(value, part[way * away, which])
            moving[way, which] = (away, value)
    sums = []
    for which in range(2):
        value = part[0, which].astype(F32)
        value = value + moving[1, which][1].astype(F32) + moving[-1, which][1].astype(F32)
        sums.append(value.astype(BF16))
    returned = lax.all_to_all(
        jnp.concatenate(sums, axis=0).reshape(experts, cap, width), "expert", 0, 0, tiled=True
    ).reshape(slots, width)
    (down_grad,) = call(
        functools.partial(down_kernel, width),
        (struct((hid, model), BF16),),
        (*chunks, hidden),
        2 * slots * model * hid,
    )
    own_moe = dot(pick, returned, FIRST).astype(BF16)
    moe = lax.all_to_all(
        jnp.broadcast_to(own_moe[None], (n, tokens, width)), "tensor", 0, 0, tiled=True
    )
    resid_grad, attn_grad = call(
        tail_kernel,
        (struct((own, model), BF16), struct((tokens, out_proj.shape[0]), BF16)),
        (moe, all_rows, all_norm, norm_gain[None], proj),
        2 * tokens * model * out_proj.shape[0],
        (pltpu.VMEM((tokens, model), F32),),
    )
    return (resid_grad[None], attn_grad[None], down_grad[None])


def solution(mesh):
    placed = (
        P("expert", "tensor", None),
        P("expert", "tensor", None),
        P(),
        P("expert", None, None),
        P("expert", None, None),
        P("expert", None, "tensor"),
        P("expert", None, "tensor"),
        P("expert", None, "tensor"),
        P("expert", None, "tensor"),
        P("expert", "tensor", None),
        P("tensor", "expert"),
    )
    return jax.shard_map(
        per_device,
        mesh=mesh,
        in_specs=placed,
        out_specs=(
            P("expert", "tensor", None),
            P("expert", None, "tensor"),
            P("expert", "tensor", None),
        ),
        check_vma=False,
    )
```

time: 394 us -> 256 us (0.65)
  blocking collectives: 163 us -> 23.5 us
  starting transfers between devices: 5.87 us -> 129 us
  waiting for transfers between devices: 162 us -> 44.6 us
  Pallas kernels: 0 us -> 10.7 us
  matrix products: 13.3 us -> 2.62 us
  other arithmetic: 9.32 us -> 2.68 us
    ppermute x0 -> x28, starting transfers between devices: none -> 99.4 us  [shift(): return lax.ppermute(x, 'tensor', [(i, (i + step) % n) for i in range(n)])]
    all_to_all x1, blocking collectives: 107 us -> 23.5 us  [per_device(): lax.all_to_all(jnp.concatenate(sums, axis=0).reshape(experts, cap, width)...]
    unnamed x3 -> x1, waiting for transfers between devices: 66.3 us -> 0.68 us
    all_to_all x1 -> x4, waiting for transfers between devices: 96 us -> 36.1 us  [the longest x1 15.4 us: per_device(): lax.all_to_all(scaled.reshape(experts, cap, width), 'expert', 0, 0, tiled...]
    all_gather x2 -> x0, blocking collectives: 56.4 us -> none  [the longest x1 31.6 us: per_device(): group_grads = lax.all_gather(out_grad, 'tensor', axis=1, tiled=True)]
    all_to_all x1 -> x4, starting transfers between devices: 5.6 us -> 29.3 us  [the longest x1 10.6 us: per_device(): lax.all_to_all(scaled.reshape(experts, cap, width), 'expert', 0, 0, tiled...]
    gather x3 -> x0, local copies, waits for them, and re-layouts: 14.5 us -> none  [the longest x1 6.61 us: per_device(): routed = returned.reshape(expert_count * slot_cap, model_width)[position]]
    pallas_call x0 -> x4, Pallas kernels: none -> 10.7 us  [call(): pl.pallas_call(kernel, out_shape=list(out_shapes), in_specs=vmem_specs(le...]
  transfers between devices with their start and end apart: 3 -> 33, of which waited for: 2 -> 8; matrix products, arithmetic and copies ran while one was open for 2% -> 7% of each run, Pallas kernels for 0% -> 3%
where the time goes in v1:
time: 256 us; the launch traced here: 251 us
  starting transfers between devices  129 us (50%)
  waiting for transfers between devices  44.6 us (17%)
  blocking collectives  23.5 us (9%)
  local copies, waits for them, and re-layouts  23.4 us (9%)
  between operations  14.7 us (6%)
  Pallas kernels  10.7 us (4%)
  other arithmetic  2.68 us (1%)
  matrix products  2.62 us (1%)
    ppermute x28, starting transfers between devices, shift(): return lax.ppermute(x, 'tensor', [(i, (i + step) % n) for i in range(n)])  99.4 us
    all_to_all x1, blocking collectives, per_device(): lax.all_to_all(jnp.concatenate(sums, axis=0).reshape(experts, cap, width)...  23.5 us
    all_to_all x1, waiting for transfers between devices, per_device(): lax.all_to_all(scaled.reshape(experts, cap, width), 'expert', 0, 0, tiled...  15.4 us
    all_to_all x1, waiting for transfers between devices, per_device(): lax.all_to_all(jnp.broadcast_to(both[None], (n, *both.shape)), 'tensor',...  15 us
    unnamed x42, local copies, waits for them, and re-layouts  12 us
    pallas_call x4, Pallas kernels, call(): pl.pallas_call(kernel, out_shape=list(out_shapes), in_specs=vmem_specs(le...  10.7 us
    all_to_all x1, starting transfers between devices, per_device(): lax.all_to_all(scaled.reshape(experts, cap, width), 'expert', 0, 0, tiled...  10.6 us
    all_to_all x1, starting transfers between devices, per_device(): own_rows = lax.all_to_all(out_grad[0], 'tensor', 1, 0, tiled=True)  10.3 us
  transfers between devices with their start and end apart: 33, of which 8 were waited for; matrix products, arithmetic and copies ran while one was open for 7% of the time, Pallas kernels for 3%

profile of v1, /device:TPU:6, one launch (start us, length us, event | category | flops | bytes accessed | tf_op | source)
XLA Modules:
  0.0 251.1 jit_solution(16228631985862554310)
XLA Ops:
  7.2 10.3 %all-to-all-start = ((bf16[4,8,512]{2,0,1:T(4,128)(2,1)}), bf16[4,8,512]{2,0,1:T(4,128)(2,1)S(1)}, u32[]{:S(2)}, u32[]{:S(2)}) async-start(bf16[4,8,512]{2,0,1:T(4,128)(2,1)} %bitcast.35), calls=%async_computation | async-start | bytes 65536 | tf_op jit(solution)/shard_map/all_to_all | solution.py:160
  17.5 0.8 copy.23
  18.5 0.8 copy.24
  19.8 5.7 %all-to-all-done = bf16[4,8,512]{2,0,1:T(4,128)(2,1)S(1)} async-done(((bf16[4,8,512]{2,0,1:T(4,128)(2,1)}), bf16[4,8,512]{2,0,1:T(4,128)(2,1)S(1)}, u32[]{:S(2)}, u32[]{:S(2)}) %all-to-all-start) | async-done | bytes 32800 | tf_op jit(solution)/shard_map/all_to_all | solution.py:160
  25.5 1.1 fusion.1
  26.7 10.6 %all-to-all-start.1 = ((bf16[64,8,512]{2,1,0:T(8,128)(2,1)}), bf16[64,8,512]{2,1,0:T(8,128)(2,1)S(1)}, u32[]{:S(2)}, u32[]{:S(2)}) async-start(bf16[64,8,512]{2,1,0:T(8,128)(2,1)} %fusion.1), calls=%async_computation.1 | async-start | bytes 1048576 | tf_op jit(solution)/shard_map/all_to_all | solution.py:162
  38.0 1.4 pad_maximum_fusion
  39.4 15.4 %all-to-all-done.1 = bf16[64,8,512]{2,1,0:T(8,128)(2,1)S(1)} async-done(((bf16[64,8,512]{2,1,0:T(8,128)(2,1)}), bf16[64,8,512]{2,1,0:T(8,128)(2,1)S(1)}, u32[]{:S(2)}, u32[]{:S(2)}) %all-to-all-start.1) | async-done | bytes 524320 | tf_op jit(solution)/shard_map/all_to_all | solution.py:162
  54.9 2.6 %collective-permute-start.2 = (bf16[256,512]{1,0:T(8,128)(2,1)S(1)}, bf16[256,512]{1,0:T(8,128)(2,1)S(1)}, u32[]{:S(2)}, u32[]{:S(2)}) collective-permute-start(bf16[256,512]{1,0:T(8,128)(2,1)S(1)} %get-tuple-element.52.refs_0_), channel_id=1, source_target_pairs={{0,64},{64,128},{128,192},{192,256},{256,320},{320,384},{384,448},... | collective-permute-start | bytes 786440 | tf_op jit(solution)/shard_map/ppermute | solution.py:115
  57.5 4.6 %collective-permute-start.1 = (bf16[256,512]{1,0:T(8,128)(2,1)S(1)}, bf16[256,512]{1,0:T(8,128)(2,1)S(1)}, u32[]{:S(2)}, u32[]{:S(2)}) collective-permute-start(bf16[256,512]{1,0:T(8,128)(2,1)S(1)} %get-tuple-element.51.refs_1_), channel_id=1, source_target_pairs={{0,448},{64,0},{128,64},{192,128},{256,192},{320,256},{384,320},{4... | collective-permute-start | bytes 786440 | tf_op jit(solution)/shard_map/ppermute | solution.py:115
  62.1 1.9 collective-permute-start.3
  64.0 5.1 %collective-permute-start = (bf16[256,512]{1,0:T(8,128)(2,1)S(1)}, bf16[256,512]{1,0:T(8,128)(2,1)S(1)}, u32[]{:S(2)}, u32[]{:S(2)}) collective-permute-start(bf16[256,512]{1,0:T(8,128)(2,1)S(1)} %get-tuple-element.52.refs_0_), channel_id=1, source_target_pairs={{0,448},{64,0},{128,64},{192,128},{256,192},{320,256},{384,320},{4... | collective-permute-start | bytes 786440 | tf_op jit(solution)/shard_map/ppermute | solution.py:115
  69.2 1.9 collective-permute-start.6
  71.1 5.1 %collective-permute-start.5 = (bf16[256,512]{1,0:T(8,128)(2,1)S(1)}, bf16[256,512]{1,0:T(8,128)(2,1)S(1)}, u32[]{:S(2)}, u32[]{:S(2)}) collective-permute-start(bf16[256,512]{1,0:T(8,128)(2,1)S(1)} %collective-permute-done.1.refs_3_), channel_id=1, source_target_pairs={{0,448},{64,0},{128,64},{192,128},{256,192},{320,256},{384,320},{4... | collective-permute-start | bytes 786440 | tf_op jit(solution)/shard_map/ppermute | solution.py:115
  76.3 1.9 collective-permute-start.7
  78.2 5.1 %collective-permute-start.4 = (bf16[256,512]{1,0:T(8,128)(2,1)S(1)}, bf16[256,512]{1,0:T(8,128)(2,1)S(1)}, u32[]{:S(2)}, u32[]{:S(2)}) collective-permute-start(bf16[256,512]{1,0:T(8,128)(2,1)S(1)} %collective-permute-done.refs_2_), channel_id=1, source_target_pairs={{0,448},{64,0},{128,64},{192,128},{256,192},{320,256},{384,320},{4... | collective-permute-start | bytes 786440 | tf_op jit(solution)/shard_map/ppermute | solution.py:115
  83.3 1.9 collective-permute-start.10
  85.3 5.1 %collective-permute-start.9 = (bf16[256,512]{1,0:T(8,128)(2,1)S(1)}, bf16[256,512]{1,0:T(8,128)(2,1)S(1)}, u32[]{:S(2)}, u32[]{:S(2)}) collective-permute-start(bf16[256,512]{1,0:T(8,128)(2,1)S(1)} %collective-permute-done.5.refs_7_), channel_id=1, source_target_pairs={{0,448},{64,0},{128,64},{192,128},{256,192},{320,256},{384,320},{4... | collective-permute-start | bytes 786440 | tf_op jit(solution)/shard_map/ppermute | solution.py:115
  90.4 1.9 collective-permute-start.11
  92.4 5.1 %collective-permute-start.8 = (bf16[256,512]{1,0:T(8,128)(2,1)S(1)}, bf16[256,512]{1,0:T(8,128)(2,1)S(1)}, u32[]{:S(2)}, u32[]{:S(2)}) collective-permute-start(bf16[256,512]{1,0:T(8,128)(2,1)S(1)} %collective-permute-done.4.refs_6_), channel_id=1, source_target_pairs={{0,448},{64,0},{128,64},{192,128},{256,192},{320,256},{384,320},{4... | collective-permute-start | bytes 786440 | tf_op jit(solution)/shard_map/ppermute | solution.py:115
  97.5 1.9 collective-permute-start.12
  99.5 5.1 %collective-permute-start.13 = (bf16[256,512]{1,0:T(8,128)(2,1)S(1)}, bf16[256,512]{1,0:T(8,128)(2,1)S(1)}, u32[]{:S(2)}, u32[]{:S(2)}) collective-permute-start(bf16[256,512]{1,0:T(8,128)(2,1)S(1)} %collective-permute-done.9.refs_11_), channel_id=1, source_target_pairs={{0,448},{64,0},{128,64},{192,128},{256,192},{320,256},{384,320},{4... | collective-permute-start | bytes 786440 | tf_op jit(solution)/shard_map/ppermute | solution.py:115
  104.7 2.3 collective-permute-done.12.refs_14_
  107.0 1.5 collective-permute-done.13.refs_15_
  108.5 1.0 copy-done.15
  109.5 0.9 copy-done.16
  110.4 4.9 %shard_map.130 = (bf16[512,128]{1,0:T(8,128)(2,1)S(1)}, bf16[512,128]{1,0:T(8,128)(2,1)S(1)}, bf16[512,128]{1,0:T(8,128)(2,1)S(1)}, bf16[256,512]{1,0:T(8,128)(2,1)S(1)}, bf16[256,512]{1,0:T(8,128)(2,1)S(1)}) custom-call(bf16[256,512]{1,0:T(8,128)(2,1)S(1)} %get-tuple-element.52.refs_0_, bf16[256,512]{1,0:T(8,128)(2,1)S(1)} %get-tuple-element.51.refs_1_, ...), custom_call_target="tpu_custom_call" | custom-call | flops 536870912 | bytes 8519680 | tf_op jit(solution)/shard_map/pallas_call | solution.py:29
  116.0 1.9 collective-permute-start.14
  117.9 2.1 shard_map.131
  120.0 5.6 %collective-permute-start.18 = (bf16[256,512]{1,0:T(8,128)(2,1)S(1)}, bf16[256,512]{1,0:T(8,128)(2,1)S(1)}, u32[]{:S(2)}, u32[]{:S(2)}) collective-permute-start(bf16[256,512]{1,0:T(8,128)(2,1)S(1)} %get-tuple-element.34), channel_id=1, source_target_pairs={{0,448},{64,0},{128,64},{192,128},{256,192},{320,256},{384,320},{4... | collective-permute-start | bytes 786440 | tf_op jit(solution)/shard_map/ppermute | solution.py:115
  125.6 1.9 collective-permute-start.21
  127.5 5.1 %collective-permute-start.24 = (bf16[256,512]{1,0:T(8,128)(2,1)S(1)}, bf16[256,512]{1,0:T(8,128)(2,1)S(1)}, u32[]{:S(2)}, u32[]{:S(2)}) collective-permute-start(bf16[256,512]{1,0:T(8,128)(2,1)S(1)} %get-tuple-element.41), channel_id=1, source_target_pairs={{0,448},{64,0},{128,64},{192,128},{256,192},{320,256},{384,320},{4... | collective-permute-start | bytes 786440 | tf_op jit(solution)/shard_map/ppermute | solution.py:115
  132.8 1.9 collective-permute-start.15
  134.8 5.1 %collective-permute-start.19 = (bf16[256,512]{1,0:T(8,128)(2,1)S(1)}, bf16[256,512]{1,0:T(8,128)(2,1)S(1)}, u32[]{:S(2)}, u32[]{:S(2)}) collective-permute-start(bf16[256,512]{1,0:T(8,128)(2,1)S(1)} %add_convert_fusion.8), channel_id=1, source_target_pairs={{0,448},{64,0},{128,64},{192,128},{256,192},{320,256},{384,320},{4... | collective-permute-start | bytes 786440 | tf_op jit(solution)/shard_map/ppermute | solution.py:115
  140.0 1.9 collective-permute-start.22
  142.0 5.1 %collective-permute-start.25 = (bf16[256,512]{1,0:T(8,128)(2,1)S(1)}, bf16[256,512]{1,0:T(8,128)(2,1)S(1)}, u32[]{:S(2)}, u32[]{:S(2)}) collective-permute-start(bf16[256,512]{1,0:T(8,128)(2,1)S(1)} %add_convert_fusion.3), channel_id=1, source_target_pairs={{0,448},{64,0},{128,64},{192,128},{256,192},{320,256},{384,320},{4... | collective-permute-start | bytes 786440 | tf_op jit(solution)/shard_map/ppermute | solution.py:115
  147.2 2.1 collective-permute-start.16
  149.4 5.1 %collective-permute-start.20 = (bf16[256,512]{1,0:T(8,128)(2,1)S(1)}, bf16[256,512]{1,0:T(8,128)(2,1)S(1)}, u32[]{:S(2)}, u32[]{:S(2)}) collective-permute-start(bf16[256,512]{1,0:T(8,128)(2,1)S(1)} %add_convert_fusion.7), channel_id=1, source_target_pairs={{0,448},{64,0},{128,64},{192,128},{256,192},{320,256},{384,320},{4... | collective-permute-start | bytes 786440 | tf_op jit(solution)/shard_map/ppermute | solution.py:115
  154.6 4.9 %collective-permute-start.26 = (bf16[256,512]{1,0:T(8,128)(2,1)S(1)}, bf16[256,512]{1,0:T(8,128)(2,1)S(1)}, u32[]{:S(2)}, u32[]{:S(2)}) collective-permute-start(bf16[256,512]{1,0:T(8,128)(2,1)S(1)} %add_convert_fusion.2), channel_id=1, source_target_pairs={{0,448},{64,0},{128,64},{192,128},{256,192},{320,256},{384,320},{4... | collective-permute-start | bytes 786440 | tf_op jit(solution)/shard_map/ppermute | solution.py:115
  159.6 1.9 collective-permute-start.17
  161.6 1.9 collective-permute-start.23
  163.8 5.4 %collective-permute-start.27 = (bf16[256,512]{1,0:T(8,128)(2,1)S(1)}, bf16[256,512]{1,0:T(8,128)(2,1)S(1)}, u32[]{:S(2)}, u32[]{:S(2)}) collective-permute-start(bf16[256,512]{1,0:T(8,128)(2,1)S(1)} %add_convert_fusion.1), channel_id=1, source_target_pairs={{0,448},{64,0},{128,64},{192,128},{256,192},{320,256},{384,320},{4... | collective-permute-start | bytes 786440 | tf_op jit(solution)/shard_map/ppermute | solution.py:115
  169.3 2.6 %collective-permute-done.23 = bf16[256,512]{1,0:T(8,128)(2,1)S(1)} collective-permute-done((bf16[256,512]{1,0:T(8,128)(2,1)S(1)}, bf16[256,512]{1,0:T(8,128)(2,1)S(1)}, u32[]{:S(2)}, u32[]{:S(2)}) %collective-permute-start.23) | collective-permute-done | bytes 262176 | tf_op jit(solution)/shard_map/ppermute | solution.py:115
  171.9 1.2 collective-permute-done.27
  173.2 23.5 %all_to_all.39 = bf16[64,8,512]{2,1,0:T(8,128)(2,1)} all-to-all(bf16[64,8,512]{2,1,0:T(8,128)(2,1)S(1)} %maximum_bitcast_fusion), channel_id=1, replica_groups=mesh['tensor'=8,'expert'=64] {'expert'}, dimensions={0} | all-to-all | bytes 1048576 | tf_op jit(solution)/shard_map/all_to_all | solution.py:226
  196.7 0.8 broadcast_in_dim.49
  197.5 5.0 %all-to-all-start.4 = ((bf16[8,8,4096]{2,1,0:T(8,128)(2,1)}), bf16[8,8,4096]{2,1,0:T(8,128)(2,1)S(1)}, u32[]{:S(2)}, u32[]{:S(2)}) async-start(bf16[8,8,4096]{2,1,0:T(8,128)(2,1)} %broadcast_in_dim.49), calls=%async_computation.4 | async-start | bytes 1048576 | tf_op jit(solution)/shard_map/all_to_all | solution.py:181
  202.5 1.2 convolution_convert_fusion.1
  203.8 15.0 %all-to-all-done.4 = bf16[8,8,4096]{2,1,0:T(8,128)(2,1)S(1)} async-done(((bf16[8,8,4096]{2,1,0:T(8,128)(2,1)}), bf16[8,8,4096]{2,1,0:T(8,128)(2,1)S(1)}, u32[]{:S(2)}, u32[]{:S(2)}) %all-to-all-start.4) | async-done | bytes 524320 | tf_op jit(solution)/shard_map/all_to_all | solution.py:181
  218.8 0.7 broadcast_in_dim.48
  219.5 3.4 %all-to-all-start.3 = ((bf16[8,32,512]{2,1,0:T(8,128)(2,1)}), bf16[8,32,512]{2,1,0:T(8,128)(2,1)S(1)}, u32[]{:S(2)}, u32[]{:S(2)}) async-start(bf16[8,32,512]{2,1,0:T(8,128)(2,1)} %broadcast_in_dim.48), calls=%async_computation.3 | async-start | bytes 524288 | tf_op jit(solution)/shard_map/all_to_all | solution.py:236
  222.9 1.0 fusion.6
  223.9 1.0 reshape.83.rows_ref
  225.0 1.0 reshape.84.norm_ref
  226.0 0.9 copy-done.4
  226.9 0.9 copy-done.6
  227.9 0.9 copy-done.8
  228.8 0.9 copy-done.10
  229.8 0.9 copy-done.12
  230.7 0.9 copy-done.14
  231.7 1.7 shard_map.133
  233.4 6.5 %copy.26.proj_ref = bf16[512,4096]{1,0:T(8,128)(2,1)} copy(bf16[512,4096]{0,1:T(8,128)(2,1)} %all-gather.2.cloned.1.call-done) | data formatting | bytes 8388608 | tf_op jit(solution)/shard_map/all_gather | solution.py:187
  239.9 2.2 copy-done
  242.1 2.1 shard_map.132
  (80 shorter events, 3.5 us)
Async XLA Ops:
  7.2 18.4 %all-to-all-start = ((bf16[4,8,512]{2,0,1:T(4,128)(2,1)}), bf16[4,8,512]{2,0,1:T(4,128)(2,1)S(1)}, u32[]{:S(2)}, u32[]{:S(2)}) async-start(bf16[4,8,512]{2,0,1:T(4,128)(2,1)} %bitcast.35), calls=%async_computation | async-start | bytes 65536 | tf_op jit(solution)/shard_map/all_to_all | solution.py:160
  19.7 35.2 %copy-start.19 = (bf16[512,32]{0,1:T(8,128)(2,1)}, bf16[512,32]{0,1:T(8,128)(2,1)S(1)}, u32[]{:S(2)}) copy-start(bf16[512,32]{0,1:T(8,128)(2,1)S(1)} %convolution_convert_fusion) | copy-start | bytes 98308
  26.7 28.2 %all-to-all-start.1 = ((bf16[64,8,512]{2,1,0:T(8,128)(2,1)}), bf16[64,8,512]{2,1,0:T(8,128)(2,1)S(1)}, u32[]{:S(2)}, u32[]{:S(2)}) async-start(bf16[64,8,512]{2,1,0:T(8,128)(2,1)} %fusion.1), calls=%async_computation.1 | async-start | bytes 1048576 | tf_op jit(solution)/shard_map/all_to_all | solution.py:162
  37.3 196.1 %all-gather.2.cloned.1.call-start = ((), (), s32[]{:S(2)}) async-start(), calls=%async_computation.5 | async-start | bytes 4259840 | tf_op jit(solution)/shard_map/all_gather | solution.py:187
  54.8 63.1 %copy-start.1 = (bf16[1,4096,128]{2,1,0:T(8,128)(2,1)S(1)}, bf16[1,4096,128]{2,1,0:T(8,128)(2,1)}, u32[]{:S(2)}) copy-start(bf16[1,4096,128]{2,1,0:T(8,128)(2,1)} %param.18) | copy-start | bytes 3145732
  54.8 63.1 %copy-start.2 = (bf16[1,4096,128]{2,1,0:T(8,128)(2,1)S(1)}, bf16[1,4096,128]{2,1,0:T(8,128)(2,1)}, u32[]{:S(2)}) copy-start(bf16[1,4096,128]{2,1,0:T(8,128)(2,1)} %param.19) | copy-start | bytes 3145732
  54.9 14.3 %collective-permute-start.2 = (bf16[256,512]{1,0:T(8,128)(2,1)S(1)}, bf16[256,512]{1,0:T(8,128)(2,1)S(1)}, u32[]{:S(2)}, u32[]{:S(2)}) collective-permute-start(bf16[256,512]{1,0:T(8,128)(2,1)S(1)} %get-tuple-element.52.refs_0_), channel_id=1, source_target_pairs={{0,64},{64,128},{128,192},{192,256},{256,320},{320,384},{384,448},... | collective-permute-start | bytes 786440 | tf_op jit(solution)/shard_map/ppermute | solution.py:115
  57.5 13.6 %collective-permute-start.1 = (bf16[256,512]{1,0:T(8,128)(2,1)S(1)}, bf16[256,512]{1,0:T(8,128)(2,1)S(1)}, u32[]{:S(2)}, u32[]{:S(2)}) collective-permute-start(bf16[256,512]{1,0:T(8,128)(2,1)S(1)} %get-tuple-element.51.refs_1_), channel_id=1, source_target_pairs={{0,448},{64,0},{128,64},{192,128},{256,192},{320,256},{384,320},{4... | collective-permute-start | bytes 786440 | tf_op jit(solution)/shard_map/ppermute | solution.py:115
  62.1 14.2 %collective-permute-start.3 = (bf16[256,512]{1,0:T(8,128)(2,1)S(1)}, bf16[256,512]{1,0:T(8,128)(2,1)S(1)}, u32[]{:S(2)}, u32[]{:S(2)}) collective-permute-start(bf16[256,512]{1,0:T(8,128)(2,1)S(1)} %get-tuple-element.51.refs_1_), channel_id=1, source_target_pairs={{0,64},{64,128},{128,192},{192,256},{256,320},{320,384},{384,448},... | collective-permute-start | bytes 786440 | tf_op jit(solution)/shard_map/ppermute | solution.py:115
  64.0 14.2 %collective-permute-start = (bf16[256,512]{1,0:T(8,128)(2,1)S(1)}, bf16[256,512]{1,0:T(8,128)(2,1)S(1)}, u32[]{:S(2)}, u32[]{:S(2)}) collective-permute-start(bf16[256,512]{1,0:T(8,128)(2,1)S(1)} %get-tuple-element.52.refs_0_), channel_id=1, source_target_pairs={{0,448},{64,0},{128,64},{192,128},{256,192},{320,256},{384,320},{4... | collective-permute-start | bytes 786440 | tf_op jit(solution)/shard_map/ppermute | solution.py:115
  69.2 14.2 %collective-permute-start.6 = (bf16[256,512]{1,0:T(8,128)(2,1)S(1)}, bf16[256,512]{1,0:T(8,128)(2,1)S(1)}, u32[]{:S(2)}, u32[]{:S(2)}) collective-permute-start(bf16[256,512]{1,0:T(8,128)(2,1)S(1)} %collective-permute-done.2.refs_4_), channel_id=1, source_target_pairs={{0,64},{64,128},{128,192},{192,256},{256,320},{320,384},{384,448},... | collective-permute-start | bytes 786440 | tf_op jit(solution)/shard_map/ppermute | solution.py:115
  71.1 14.2 %collective-permute-start.5 = (bf16[256,512]{1,0:T(8,128)(2,1)S(1)}, bf16[256,512]{1,0:T(8,128)(2,1)S(1)}, u32[]{:S(2)}, u32[]{:S(2)}) collective-permute-start(bf16[256,512]{1,0:T(8,128)(2,1)S(1)} %collective-permute-done.1.refs_3_), channel_id=1, source_target_pairs={{0,448},{64,0},{128,64},{192,128},{256,192},{320,256},{384,320},{4... | collective-permute-start | bytes 786440 | tf_op jit(solution)/shard_map/ppermute | solution.py:115
  76.3 14.2 %collective-permute-start.7 = (bf16[256,512]{1,0:T(8,128)(2,1)S(1)}, bf16[256,512]{1,0:T(8,128)(2,1)S(1)}, u32[]{:S(2)}, u32[]{:S(2)}) collective-permute-start(bf16[256,512]{1,0:T(8,128)(2,1)S(1)} %collective-permute-done.3.refs_5_), channel_id=1, source_target_pairs={{0,64},{64,128},{128,192},{192,256},{256,320},{320,384},{384,448},... | collective-permute-start | bytes 786440 | tf_op jit(solution)/shard_map/ppermute | solution.py:115
  78.2 14.2 %collective-permute-start.4 = (bf16[256,512]{1,0:T(8,128)(2,1)S(1)}, bf16[256,512]{1,0:T(8,128)(2,1)S(1)}, u32[]{:S(2)}, u32[]{:S(2)}) collective-permute-start(bf16[256,512]{1,0:T(8,128)(2,1)S(1)} %collective-permute-done.refs_2_), channel_id=1, source_target_pairs={{0,448},{64,0},{128,64},{192,128},{256,192},{320,256},{384,320},{4... | collective-permute-start | bytes 786440 | tf_op jit(solution)/shard_map/ppermute | solution.py:115
  83.3 14.2 %collective-permute-start.10 = (bf16[256,512]{1,0:T(8,128)(2,1)S(1)}, bf16[256,512]{1,0:T(8,128)(2,1)S(1)}, u32[]{:S(2)}, u32[]{:S(2)}) collective-permute-start(bf16[256,512]{1,0:T(8,128)(2,1)S(1)} %collective-permute-done.6.refs_8_), channel_id=1, source_target_pairs={{0,64},{64,128},{128,192},{192,256},{256,320},{320,384},{384,448},... | collective-permute-start | bytes 786440 | tf_op jit(solution)/shard_map/ppermute | solution.py:115
  85.3 14.2 %collective-permute-start.9 = (bf16[256,512]{1,0:T(8,128)(2,1)S(1)}, bf16[256,512]{1,0:T(8,128)(2,1)S(1)}, u32[]{:S(2)}, u32[]{:S(2)}) collective-permute-start(bf16[256,512]{1,0:T(8,128)(2,1)S(1)} %collective-permute-done.5.refs_7_), channel_id=1, source_target_pairs={{0,448},{64,0},{128,64},{192,128},{256,192},{320,256},{384,320},{4... | collective-permute-start | bytes 786440 | tf_op jit(solution)/shard_map/ppermute | solution.py:115
  90.4 14.2 %collective-permute-start.11 = (bf16[256,512]{1,0:T(8,128)(2,1)S(1)}, bf16[256,512]{1,0:T(8,128)(2,1)S(1)}, u32[]{:S(2)}, u32[]{:S(2)}) collective-permute-start(bf16[256,512]{1,0:T(8,128)(2,1)S(1)} %collective-permute-done.7.refs_9_), channel_id=1, source_target_pairs={{0,64},{64,128},{128,192},{192,256},{256,320},{320,384},{384,448},... | collective-permute-start | bytes 786440 | tf_op jit(solution)/shard_map/ppermute | solution.py:115
  92.4 12.3 %collective-permute-start.8 = (bf16[256,512]{1,0:T(8,128)(2,1)S(1)}, bf16[256,512]{1,0:T(8,128)(2,1)S(1)}, u32[]{:S(2)}, u32[]{:S(2)}) collective-permute-start(bf16[256,512]{1,0:T(8,128)(2,1)S(1)} %collective-permute-done.4.refs_6_), channel_id=1, source_target_pairs={{0,448},{64,0},{128,64},{192,128},{256,192},{320,256},{384,320},{4... | collective-permute-start | bytes 786440 | tf_op jit(solution)/shard_map/ppermute | solution.py:115
  97.5 9.5 %collective-permute-start.12 = (bf16[256,512]{1,0:T(8,128)(2,1)S(1)}, bf16[256,512]{1,0:T(8,128)(2,1)S(1)}, u32[]{:S(2)}, u32[]{:S(2)}) collective-permute-start(bf16[256,512]{1,0:T(8,128)(2,1)S(1)} %collective-permute-done.10.refs_12_), channel_id=1, source_target_pairs={{0,64},{64,128},{128,192},{192,256},{256,320},{320,384},{384,448},... | collective-permute-start | bytes 786440 | tf_op jit(solution)/shard_map/ppermute | solution.py:115
  99.5 15.8 %copy-start.5 = (bf16[256,512]{1,0:T(8,128)(2,1)}, bf16[256,512]{1,0:T(8,128)(2,1)S(1)}, u32[]{:S(2)}) copy-start(bf16[256,512]{1,0:T(8,128)(2,1)S(1)} %collective-permute-done.9.refs_11_) | copy-start | bytes 786436
  99.5 9.0 %collective-permute-start.13 = (bf16[256,512]{1,0:T(8,128)(2,1)S(1)}, bf16[256,512]{1,0:T(8,128)(2,1)S(1)}, u32[]{:S(2)}, u32[]{:S(2)}) collective-permute-start(bf16[256,512]{1,0:T(8,128)(2,1)S(1)} %collective-permute-done.9.refs_11_), channel_id=1, source_target_pairs={{0,448},{64,0},{128,64},{192,128},{256,192},{320,256},{384,320},{4... | collective-permute-start | bytes 786440 | tf_op jit(solution)/shard_map/ppermute | solution.py:115
  104.6 11.3 %copy-start.7 = (bf16[256,512]{1,0:T(8,128)(2,1)}, bf16[256,512]{1,0:T(8,128)(2,1)S(1)}, u32[]{:S(2)}) copy-start(bf16[256,512]{1,0:T(8,128)(2,1)S(1)} %collective-permute-done.11.refs_13_) | copy-start | bytes 786436
  104.6 13.2 %copy-start.9 = (bf16[256,512]{1,0:T(8,128)(2,1)}, bf16[256,512]{1,0:T(8,128)(2,1)S(1)}, u32[]{:S(2)}) copy-start(bf16[256,512]{1,0:T(8,128)(2,1)S(1)} %collective-permute-done.8.refs_10_) | copy-start | bytes 786436
  107.0 10.9 %copy-start.11 = (bf16[256,512]{1,0:T(8,128)(2,1)}, bf16[256,512]{1,0:T(8,128)(2,1)S(1)}, u32[]{:S(2)}) copy-start(bf16[256,512]{1,0:T(8,128)(2,1)S(1)} %collective-permute-done.12.refs_14_) | copy-start | bytes 786436
  108.5 9.4 %copy-start.13 = (bf16[256,512]{1,0:T(8,128)(2,1)}, bf16[256,512]{1,0:T(8,128)(2,1)S(1)}, u32[]{:S(2)}) copy-start(bf16[256,512]{1,0:T(8,128)(2,1)S(1)} %collective-permute-done.13.refs_15_) | copy-start | bytes 786436
  108.5 1.0 copy-start.15
  109.5 0.9 copy-start.16
  115.3 0.7 copy-start.3
  116.0 16.7 %collective-permute-start.14 = (bf16[256,512]{1,0:T(8,128)(2,1)S(1)}, bf16[256,512]{1,0:T(8,128)(2,1)S(1)}, u32[]{:S(2)}, u32[]{:S(2)}) collective-permute-start(bf16[256,512]{1,0:T(8,128)(2,1)S(1)} %get-tuple-element.30), channel_id=1, source_target_pairs={{0,64},{64,128},{128,192},{192,256},{256,320},{320,384},{384,448},... | collective-permute-start | bytes 786440 | tf_op jit(solution)/shard_map/ppermute | solution.py:115
  120.0 14.7 %collective-permute-start.18 = (bf16[256,512]{1,0:T(8,128)(2,1)S(1)}, bf16[256,512]{1,0:T(8,128)(2,1)S(1)}, u32[]{:S(2)}, u32[]{:S(2)}) collective-permute-start(bf16[256,512]{1,0:T(8,128)(2,1)S(1)} %get-tuple-element.34), channel_id=1, source_target_pairs={{0,448},{64,0},{128,64},{192,128},{256,192},{320,256},{384,320},{4... | collective-permute-start | bytes 786440 | tf_op jit(solution)/shard_map/ppermute | solution.py:115
  125.6 14.3 %collective-permute-start.21 = (bf16[256,512]{1,0:T(8,128)(2,1)S(1)}, bf16[256,512]{1,0:T(8,128)(2,1)S(1)}, u32[]{:S(2)}, u32[]{:S(2)}) collective-permute-start(bf16[256,512]{1,0:T(8,128)(2,1)S(1)} %get-tuple-element.38), channel_id=1, source_target_pairs={{0,64},{64,128},{128,192},{192,256},{256,320},{320,384},{384,448},... | collective-permute-start | bytes 786440 | tf_op jit(solution)/shard_map/ppermute | solution.py:115
  127.5 14.4 %collective-permute-start.24 = (bf16[256,512]{1,0:T(8,128)(2,1)S(1)}, bf16[256,512]{1,0:T(8,128)(2,1)S(1)}, u32[]{:S(2)}, u32[]{:S(2)}) collective-permute-start(bf16[256,512]{1,0:T(8,128)(2,1)S(1)} %get-tuple-element.41), channel_id=1, source_target_pairs={{0,448},{64,0},{128,64},{192,128},{256,192},{320,256},{384,320},{4... | collective-permute-start | bytes 786440 | tf_op jit(solution)/shard_map/ppermute | solution.py:115
  132.8 14.4 %collective-permute-start.15 = (bf16[256,512]{1,0:T(8,128)(2,1)S(1)}, bf16[256,512]{1,0:T(8,128)(2,1)S(1)}, u32[]{:S(2)}, u32[]{:S(2)}) collective-permute-start(bf16[256,512]{1,0:T(8,128)(2,1)S(1)} %add_convert_fusion.11), channel_id=1, source_target_pairs={{0,64},{64,128},{128,192},{192,256},{256,320},{320,384},{384,448},... | collective-permute-start | bytes 786440 | tf_op jit(solution)/shard_map/ppermute | solution.py:115
  134.8 14.5 %collective-permute-start.19 = (bf16[256,512]{1,0:T(8,128)(2,1)S(1)}, bf16[256,512]{1,0:T(8,128)(2,1)S(1)}, u32[]{:S(2)}, u32[]{:S(2)}) collective-permute-start(bf16[256,512]{1,0:T(8,128)(2,1)S(1)} %add_convert_fusion.8), channel_id=1, source_target_pairs={{0,448},{64,0},{128,64},{192,128},{256,192},{320,256},{384,320},{4... | collective-permute-start | bytes 786440 | tf_op jit(solution)/shard_map/ppermute | solution.py:115
  140.0 21.5 %collective-permute-start.22 = (bf16[256,512]{1,0:T(8,128)(2,1)S(1)}, bf16[256,512]{1,0:T(8,128)(2,1)S(1)}, u32[]{:S(2)}, u32[]{:S(2)}) collective-permute-start(bf16[256,512]{1,0:T(8,128)(2,1)S(1)} %add_convert_fusion.5), channel_id=1, source_target_pairs={{0,64},{64,128},{128,192},{192,256},{256,320},{320,384},{384,448},... | collective-permute-start | bytes 786440 | tf_op jit(solution)/shard_map/ppermute | solution.py:115
  142.0 12.5 %collective-permute-start.25 = (bf16[256,512]{1,0:T(8,128)(2,1)S(1)}, bf16[256,512]{1,0:T(8,128)(2,1)S(1)}, u32[]{:S(2)}, u32[]{:S(2)}) collective-permute-start(bf16[256,512]{1,0:T(8,128)(2,1)S(1)} %add_convert_fusion.3), channel_id=1, source_target_pairs={{0,448},{64,0},{128,64},{192,128},{256,192},{320,256},{384,320},{4... | collective-permute-start | bytes 786440 | tf_op jit(solution)/shard_map/ppermute | solution.py:115
  147.2 49.5 %copy-start.18 = (bf16[8,4096]{1,0:T(8,128)(2,1)S(1)}, bf16[8,4096]{1,0:T(8,128)(2,1)}, u32[]{:S(2)}) copy-start(bf16[8,4096]{1,0:T(8,128)(2,1)} %pad_maximum_fusion) | copy-start | bytes 196612
  147.2 12.3 %collective-permute-start.16 = (bf16[256,512]{1,0:T(8,128)(2,1)S(1)}, bf16[256,512]{1,0:T(8,128)(2,1)S(1)}, u32[]{:S(2)}, u32[]{:S(2)}) collective-permute-start(bf16[256,512]{1,0:T(8,128)(2,1)S(1)} %add_convert_fusion.10), channel_id=1, source_target_pairs={{0,64},{64,128},{128,192},{192,256},{256,320},{320,384},{384,448},... | collective-permute-start | bytes 786440 | tf_op jit(solution)/shard_map/ppermute | solution.py:115
  149.4 19.8 %collective-permute-start.20 = (bf16[256,512]{1,0:T(8,128)(2,1)S(1)}, bf16[256,512]{1,0:T(8,128)(2,1)S(1)}, u32[]{:S(2)}, u32[]{:S(2)}) collective-permute-start(bf16[256,512]{1,0:T(8,128)(2,1)S(1)} %add_convert_fusion.7), channel_id=1, source_target_pairs={{0,448},{64,0},{128,64},{192,128},{256,192},{320,256},{384,320},{4... | collective-permute-start | bytes 786440 | tf_op jit(solution)/shard_map/ppermute | solution.py:115
  154.6 9.1 %collective-permute-start.26 = (bf16[256,512]{1,0:T(8,128)(2,1)S(1)}, bf16[256,512]{1,0:T(8,128)(2,1)S(1)}, u32[]{:S(2)}, u32[]{:S(2)}) collective-permute-start(bf16[256,512]{1,0:T(8,128)(2,1)S(1)} %add_convert_fusion.2), channel_id=1, source_target_pairs={{0,448},{64,0},{128,64},{192,128},{256,192},{320,256},{384,320},{4... | collective-permute-start | bytes 786440 | tf_op jit(solution)/shard_map/ppermute | solution.py:115
  159.6 9.6 %collective-permute-start.17 = (bf16[256,512]{1,0:T(8,128)(2,1)S(1)}, bf16[256,512]{1,0:T(8,128)(2,1)S(1)}, u32[]{:S(2)}, u32[]{:S(2)}) collective-permute-start(bf16[256,512]{1,0:T(8,128)(2,1)S(1)} %add_convert_fusion.9), channel_id=1, source_target_pairs={{0,64},{64,128},{128,192},{192,256},{256,320},{320,384},{384,448},... | collective-permute-start | bytes 786440 | tf_op jit(solution)/shard_map/ppermute | solution.py:115
  161.6 10.3 %collective-permute-start.23 = (bf16[256,512]{1,0:T(8,128)(2,1)S(1)}, bf16[256,512]{1,0:T(8,128)(2,1)S(1)}, u32[]{:S(2)}, u32[]{:S(2)}) collective-permute-start(bf16[256,512]{1,0:T(8,128)(2,1)S(1)} %add_convert_fusion.4), channel_id=1, source_target_pairs={{0,64},{64,128},{128,192},{192,256},{256,320},{320,384},{384,448},... | collective-permute-start | bytes 786440 | tf_op jit(solution)/shard_map/ppermute | solution.py:115
  163.8 9.3 %collective-permute-start.27 = (bf16[256,512]{1,0:T(8,128)(2,1)S(1)}, bf16[256,512]{1,0:T(8,128)(2,1)S(1)}, u32[]{:S(2)}, u32[]{:S(2)}) collective-permute-start(bf16[256,512]{1,0:T(8,128)(2,1)S(1)} %add_convert_fusion.1), channel_id=1, source_target_pairs={{0,448},{64,0},{128,64},{192,128},{256,192},{320,256},{384,320},{4... | collective-permute-start | bytes 786440 | tf_op jit(solution)/shard_map/ppermute | solution.py:115
  197.5 21.2 %all-to-all-start.4 = ((bf16[8,8,4096]{2,1,0:T(8,128)(2,1)}), bf16[8,8,4096]{2,1,0:T(8,128)(2,1)S(1)}, u32[]{:S(2)}, u32[]{:S(2)}) async-start(bf16[8,8,4096]{2,1,0:T(8,128)(2,1)} %broadcast_in_dim.49), calls=%async_computation.4 | async-start | bytes 1048576 | tf_op jit(solution)/shard_map/all_to_all | solution.py:181
  219.5 20.4 %all-to-all-start.3 = ((bf16[8,32,512]{2,1,0:T(8,128)(2,1)}), bf16[8,32,512]{2,1,0:T(8,128)(2,1)S(1)}, u32[]{:S(2)}, u32[]{:S(2)}) async-start(bf16[8,32,512]{2,1,0:T(8,128)(2,1)} %broadcast_in_dim.48), calls=%async_computation.3 | async-start | bytes 524288 | tf_op jit(solution)/shard_map/all_to_all | solution.py:236
  226.0 1.0 copy-start.4
  226.9 0.9 copy-start.6
  227.9 0.9 copy-start.8
  228.8 0.9 copy-start.10
  229.8 0.9 copy-start.12
  230.7 0.9 copy-start.14
  233.4 6.5 %copy-start.17 = (f32[4096]{0:T(1024)S(1)}, f32[4096]{0:T(1024)}, u32[]{:S(2)}) copy-start(f32[4096]{0:T(1024)} %param.13) | copy-start | bytes 49156
  239.9 2.2 copy-start
Sparse Core Ops, SparseCore 0:
  41.4 78.6 all-gather.1

commit v2 on v1

v2 whole, which is shorter than its diff:
```python
import functools
import math

import jax
import jax.numpy as jnp
from jax import lax
from jax.experimental import pallas as pl
from jax.experimental.pallas import tpu as pltpu
from jax.sharding import PartitionSpec as P

F32 = jnp.float32
BF16 = jnp.bfloat16
LAST = (((1,), (1,)), ((), ()))
FIRST = (((0,), (0,)), ((), ()))
PLAIN = (((1,), (0,)), ((), ()))
VMEM_BYTES = 16 * 1024 * 1024
OFFSETS = (0, 1, -1, 2, -2, 3, -3, 4)


def dot(a, b, dims):
    return lax.dot_general(a, b, dims, preferred_element_type=F32)


def vmem_specs(count):
    return [pl.BlockSpec(memory_space=pltpu.VMEM)] * count


def call(kernel, out_shapes, args, flops, scratch=(), out_specs=None):
    moved = sum(math.prod(a.shape) * a.dtype.itemsize for a in (*args, *out_shapes))
    return pl.pallas_call(
        kernel,
        out_shape=list(out_shapes),
        in_specs=vmem_specs(len(args)),
        out_specs=out_specs or vmem_specs(len(out_shapes)),
        scratch_shapes=list(scratch),
        compiler_params=pltpu.CompilerParams(vmem_limit_bytes=VMEM_BYTES),
        cost_estimate=pl.CostEstimate(flops=flops, bytes_accessed=moved, transcendentals=0),
    )(*args)


def struct(shape, dtype):
    return jax.ShapeDtypeStruct(shape, dtype)


def slice_at(offset, width):
    n = lax.axis_size("tensor")
    index = lax.rem(lax.axis_index("tensor") + (offset + n), n)
    return pl.ds(pl.multiple_of(index * width, width), width)


def ready_kernel(
    gate_ref, up_ref, w_down, w_gate, w_up, slope_ref, act_ref, hidden_ref, down_ref, side_ref
):
    gate = gate_ref[...].astype(F32)
    upper = up_ref[...].astype(F32)
    sig = jax.nn.sigmoid(gate)
    act = gate * sig
    slope_ref[...] = upper * sig * (1.0 + gate * (1.0 - sig))
    act_ref[...] = act
    hidden_ref[...] = (act * upper).T.astype(BF16)
    hid = w_gate.shape[1]
    down_ref[...] = w_down[...].T
    side_ref[:hid, :] = w_gate[...].T
    side_ref[hid:, :] = w_up[...].T


def early_kernel(width, *refs):
    chunks = refs[:14]
    hidden, down_ref, total_ref, out = refs[14:]
    rows = chunks[0].shape[0]
    for half in range(2):
        total = None
        for k, offset in enumerate(OFFSETS[:7]):
            term = dot(chunks[2 * k + half][...], down_ref[slice_at(offset, width), :], PLAIN)
            total = term if total is None else total + term
        total_ref[pl.ds(half * rows, rows), :] = total
    for k, offset in enumerate(OFFSETS[:7]):
        down = dot(hidden[:, :rows], chunks[2 * k][...], PLAIN)
        down = down + dot(hidden[:, rows:], chunks[2 * k + 1][...], PLAIN)
        out[:, slice_at(offset, width)] = down.astype(BF16)


def late_kernel(width, *refs):
    chunks, (hidden, total_ref, slope_ref, act_ref, down_ref, side_ref) = refs[:2], refs[2:8]
    part_hbm, out, grads_ref, part_ref, sems = refs[8:]
    rows = chunks[0].shape[0]
    hid = slope_ref.shape[1]
    cols = slice_at(OFFSETS[7], width)
    for half in range(2):
        here = pl.ds(half * rows, rows)
        total = total_ref[here, :] + dot(chunks[half][...], down_ref[cols, :], PLAIN)
        grads_ref[here, :hid] = (total * slope_ref[here, :]).astype(BF16)
        grads_ref[here, hid:] = (total * act_ref[here, :]).astype(BF16)
    copies = []
    for j in range(part_ref.shape[0]):
        for half in range(2):
            here = pl.ds(half * rows, rows)
            part = dot(grads_ref[here, :], side_ref[:, pl.ds(j * width, width)], PLAIN)
            part_ref[j, here, :] = part.astype(BF16)
        copies.append(pltpu.make_async_copy(part_ref.at[j], part_hbm.at[j], sems.at[j]))
        copies[-1].start()
    down = dot(hidden[:, :rows], chunks[0][...], PLAIN)
    down = down + dot(hidden[:, rows:], chunks[1][...], PLAIN)
    out[...] = down.astype(BF16)
    for copy in copies:
        copy.wait()


def token_kernel(pick_ref, slot_ref, out_ref):
    total = dot(pick_ref[...], slot_ref[...], FIRST).astype(BF16)
    for j in range(out_ref.shape[0]):
        out_ref[j] = total


def tail_kernel(moe_ref, rows_ref, norm_ref, gain_ref, proj_ref, resid_ref, attn_ref, held):
    n, _, width = moe_ref.shape
    model = n * width
    norm_in = norm_ref[...].astype(F32)
    inv = lax.rsqrt(jnp.sum(norm_in * norm_in, axis=-1, keepdims=True) / model + 1e-06)
    moe = jnp.concatenate([moe_ref[j] for j in range(n)], axis=1).astype(F32)
    scaled = gain_ref[...] * moe
    along = jnp.sum(scaled * norm_in, axis=-1, keepdims=True)
    resid = rows_ref[...].astype(F32) + inv * scaled - inv * inv * inv / model * norm_in * along
    held[...] = resid
    attn_ref[...] = dot(resid.astype(BF16), proj_ref[...], PLAIN).astype(BF16)
    own = resid_ref.shape[0]
    index = lax.axis_index("tensor")
    pair = held[pl.ds(pl.multiple_of(index // 2 * 2 * own, 2 * own), 2 * own), :]
    resid_ref[...] = jnp.where(lax.rem(index, 2) == 0, pair[:own], pair[own:]).astype(BF16)


def shift(x, step):
    n = lax.axis_size("tensor")
    return lax.ppermute(x, "tensor", [(i, (i + step) % n) for i in range(n)])


def per_device(
    out_grad,
    norm_input,
    norm_gain,
    routes,
    route_weight,
    gate_saved,
    up_saved,
    w_gate,
    w_up,
    w_down,
    out_proj,
):
    experts = lax.axis_size("expert")
    n = lax.axis_size("tensor")
    tokens, top = routes.shape[1:]
    slots = gate_saved.shape[1]
    cap = slots // experts
    hid = gate_saved.shape[2]
    model = out_grad.shape[2]
    width = model // n
    total = tokens * top
    half = slots // 2

    ids = routes[0].reshape(total)
    number = jnp.arange(total, dtype=jnp.int32)
    same = (ids[:, None] == ids[None, :]) & (number[None, :] < number[:, None])
    rank = jnp.sum(same.astype(jnp.int32), axis=1)
    position = ids * cap + rank
    named = position[None, :] == jnp.arange(slots, dtype=jnp.int32)[:, None]
    slot_weight = jnp.sum(
        jnp.where(named, route_weight[0].reshape(1, total), 0.0), axis=1, keepdims=True
    )
    of_token = (
        number[:, None] // top == jnp.arange(tokens, dtype=jnp.int32)[None, :]
    ).astype(BF16)
    pick = dot(named.astype(BF16), of_token, PLAIN).astype(BF16)

    own_rows = lax.all_to_all(out_grad[0], "tensor", 1, 0, tiled=True)
    scaled = (slot_weight * dot(pick, own_rows, PLAIN)).astype(BF16)
    own_slots = lax.all_to_all(
        scaled.reshape(experts, cap, width), "expert", 0, 0, tiled=True
    ).reshape(slots, width)

    own = out_grad.shape[1]
    both = jnp.concatenate([out_grad[0], norm_input[0]] * 2, axis=0)
    proj = lax.all_gather(out_proj.T, "expert", axis=0, tiled=True)
    wide = struct((slots, hid), F32)
    prepared = call(
        ready_kernel,
        (
            wide,
            wide,
            struct((hid, slots), BF16),
            struct((model, hid), BF16),
            struct((2 * hid, model), BF16),
        ),
        (gate_saved[0], up_saved[0], w_down[0], w_gate[0], w_up[0]),
        0,
    )
    own_slots, prepared, both = lax.optimization_barrier((own_slots, prepared, both))
    slope, act, hidden, down_t, side_t = prepared
    held = {(0, 0): own_slots[:half], (0, 1): own_slots[half:]}
    for step in range(1, 5):
        held[step, 0] = shift(held[step - 1, 0], 1)
        held[-step, 1] = shift(held[1 - step, 1], -1)
        if step < 4:
            held[step, 1] = shift(held[step - 1, 1], 1)
            held[-step, 0] = shift(held[1 - step, 0], -1)
    chunks = []
    for offset in OFFSETS:
        for which in range(2):
            key = -offset if offset != 4 else (4 if which == 0 else -4)
            chunks.append(held[key, which])

    total, down_grad = call(
        functools.partial(early_kernel, width),
        (struct((slots, hid), F32), struct((hid, model), BF16)),
        (*chunks[:14], hidden, down_t),
        4 * slots * model * hid,
    )
    part, last_down = call(
        functools.partial(late_kernel, width),
        (pltpu.HBM((n, slots, width), BF16), struct((hid, width), BF16)),
        (*chunks[14:], hidden, total, slope, act, down_t, side_t),
        4 * slots * model * hid,
        (
            pltpu.VMEM((slots, 2 * hid), BF16),
            pltpu.VMEM((n, slots, width), BF16),
            pltpu.SemaphoreType.DMA((n,)),
        ),
        [pl.BlockSpec(memory_space=pltpu.HBM), *vmem_specs(1)],
    )
    part, proj = lax.optimization_barrier((part, proj))
    sums = lax.psum_scatter(
        part.reshape(n * slots, width), "tensor", scatter_dimension=0, tiled=True
    )
    last = lax.rem(lax.axis_index("tensor") + OFFSETS[7], n) * width
    down_grad = lax.dynamic_update_slice(down_grad, last_down, (0, last))
    sums, both, down_grad = lax.optimization_barrier((sums, both, down_grad))
    every = lax.all_gather(both, "tensor", axis=0)
    all_rows = every[:, :own].reshape(tokens, model)
    all_norm = every[:, own : 2 * own].reshape(tokens, model)
    returned = lax.all_to_all(
        sums.reshape(experts, cap, width), "expert", 0, 0, tiled=True
    ).reshape(slots, width)
    (own_moe,) = call(
        token_kernel,
        (struct((n, tokens, width), BF16),),
        (pick, returned),
        2 * tokens * slots * width,
    )
    moe = lax.all_to_all(own_moe, "tensor", 0, 0, tiled=True)
    resid_grad, attn_grad = call(
        tail_kernel,
        (struct((own, model), BF16), struct((tokens, out_proj.shape[0]), BF16)),
        (moe, all_rows, all_norm, norm_gain[None], proj),
        2 * tokens * model * out_proj.shape[0],
        (pltpu.VMEM((tokens, model), F32),),
    )
    return (resid_grad[None], attn_grad[None], down_grad[None])


def solution(mesh):
    placed = (
        P("expert", "tensor", None),
        P("expert", "tensor", None),
        P(),
        P("expert", None, None),
        P("expert", None, None),
        P("expert", None, "tensor"),
        P("expert", None, "tensor"),
        P("expert", None, "tensor"),
        P("expert", None, "tensor"),
        P("expert", "tensor", None),
        P("tensor", "expert"),
    )
    return jax.shard_map(
        per_device,
        mesh=mesh,
        in_specs=placed,
        out_specs=(
            P("expert", "tensor", None),
            P("expert", None, "tensor"),
            P("expert", "tensor", None),
        ),
        check_vma=False,
    )
```

time: 256 us -> 222 us (0.87); the launches traced: 251 us -> 220 us
  starting transfers between devices: 129 us -> 71.1 us
  waiting for transfers between devices: 44.6 us -> 81.7 us
  local copies, waits for them, and re-layouts: 23.4 us -> 14.3 us
  blocking collectives: 23.5 us -> 27.8 us
    ppermute x28 -> x14, starting transfers between devices: 99.4 us -> 45.7 us  [shift(): return lax.ppermute(x, 'tensor', [(i, (i + step) % n) for i in range(n)])]
    reduce_scatter x0 -> x1, waiting for transfers between devices: none -> 53.5 us  [per_device(): lax.psum_scatter(part.reshape(n * slots, width), 'tensor', scatter_dimens...]
    all_to_all x2 -> x1, waiting for transfers between devices: 15 us -> 0.01 us  [per_device(): moe = lax.all_to_all(own_moe, 'tensor', 0, 0, tiled=True)]
    all_gather x1 -> x2, waiting for transfers between devices: 0.01 us -> 10.7 us  [the longest x1 10.7 us: per_device(): every = lax.all_gather(both, 'tensor', axis=0)]
    all_gather x1 -> x0, local copies, waits for them, and re-layouts: 6.52 us -> none  [per_device(): proj = lax.all_gather(out_proj, 'expert', axis=1, tiled=True)]
    ppermute x28 -> x14, waiting for transfers between devices: 7.82 us -> 1.31 us  [shift(): return lax.ppermute(x, 'tensor', [(i, (i + step) % n) for i in range(n)])]
    all_to_all x1, waiting for transfers between devices: 15.4 us -> 9.78 us  [per_device(): lax.all_to_all(scaled.reshape(experts, cap, width), 'expert', 0, 0, tiled...]
    all_to_all x1, blocking collectives: 23.5 us -> 27.8 us  [per_device(): lax.all_to_all(sums.reshape(experts, cap, width), 'expert', 0, 0, tiled=T...]
  transfers between devices with their start and end apart: 33 -> 20, of which waited for: 8 -> 6; matrix products, arithmetic and copies ran while one was open for 7% -> 3% of each run, Pallas kernels for 3% -> 3%
where the time goes in v2:
time: 222 us; the launch traced here: 220 us
  waiting for transfers between devices  81.7 us (37%)
  starting transfers between devices  71.1 us (32%)
  blocking collectives  27.8 us (13%)
  local copies, waits for them, and re-layouts  14.3 us (6%)
  between operations  14.1 us (6%)
  Pallas kernels  8.62 us (4%)
    reduce_scatter x1, waiting for transfers between devices, per_device(): lax.psum_scatter(part.reshape(n * slots, width), 'tensor', scatter_dimens...  53.5 us
    ppermute x14, starting transfers between devices, shift(): return lax.ppermute(x, 'tensor', [(i, (i + step) % n) for i in range(n)])  45.7 us
    all_to_all x1, blocking collectives, per_device(): lax.all_to_all(sums.reshape(experts, cap, width), 'expert', 0, 0, tiled=T...  27.8 us
    all_to_all x1, starting transfers between devices, per_device(): lax.all_to_all(scaled.reshape(experts, cap, width), 'expert', 0, 0, tiled...  10.8 us
    all_gather x1, waiting for transfers between devices, per_device(): every = lax.all_gather(both, 'tensor', axis=0)  10.7 us
    unnamed x28, local copies, waits for them, and re-layouts  10.6 us
    all_to_all x1, starting transfers between devices, per_device(): own_rows = lax.all_to_all(out_grad[0], 'tensor', 1, 0, tiled=True)  10.3 us
    all_to_all x1, waiting for transfers between devices, per_device(): lax.all_to_all(scaled.reshape(experts, cap, width), 'expert', 0, 0, tiled...  9.78 us
  transfers between devices with their start and end apart: 20, of which 6 were waited for; matrix products, arithmetic and copies ran while one was open for 3% of the time, Pallas kernels for 3%

profile of v2, /device:TPU:6, one launch (start us, length us, event | category | flops | bytes accessed | tf_op | source)
XLA Modules:
  0.0 220.1 jit_solution(2348542379068156084)
XLA Ops:
  7.2 0.0 all-gather.4.cloned.1.call-start
  7.2 0.7 all-gather.4.cloned.1.call-update
  7.9 10.3 %all-to-all-start = ((bf16[4,8,512]{2,0,1:T(4,128)(2,1)}), bf16[4,8,512]{2,0,1:T(4,128)(2,1)S(1)}, u32[]{:S(2)}, u32[]{:S(2)}) async-start(bf16[4,8,512]{2,0,1:T(4,128)(2,1)} %bitcast.34), calls=%async_computation | async-start | bytes 65536 | tf_op jit(solution)/shard_map/all_to_all | solution.py:175
  18.2 0.8 copy.19
  19.0 0.1 reshape_squeeze.4
  19.1 0.8 copy.21
  19.9 0.1 broadcast_in_dim.33
  20.0 0.2 convert_reduce_fusion
  20.1 0.3 convolution_convert_fusion.pick_ref
  20.5 0.2 select_reduce_fusion
  20.6 5.7 %all-to-all-done = bf16[4,8,512]{2,0,1:T(4,128)(2,1)S(1)} async-done(((bf16[4,8,512]{2,0,1:T(4,128)(2,1)}), bf16[4,8,512]{2,0,1:T(4,128)(2,1)S(1)}, u32[]{:S(2)}, u32[]{:S(2)}) %all-to-all-start) | async-done | bytes 32800 | tf_op jit(solution)/shard_map/all_to_all | solution.py:175
  26.3 1.1 fusion.1
  27.4 10.8 %all-to-all-start.1 = ((bf16[64,8,512]{2,1,0:T(8,128)(2,1)}), bf16[64,8,512]{2,1,0:T(8,128)(2,1)}, u32[]{:S(2)}, u32[]{:S(2)}) async-start(bf16[64,8,512]{2,1,0:T(8,128)(2,1)} %fusion.1), calls=%async_computation.1 | async-start | bytes 1048576 | tf_op jit(solution)/shard_map/all_to_all | solution.py:177
  38.2 0.0 reduce-scatter.2.cloned.1.call-start
  38.2 0.0 copy-start.1
  38.2 1.2 copy-done.1
  39.4 1.2 copy-done.2
  40.7 1.2 copy-done.3
  41.9 0.9 copy-done.8
  42.8 0.9 copy-done.9
  43.7 1.0 shard_map.130
  44.7 0.7 copy-done.4
  45.4 0.7 copy-done.6
  46.1 0.7 pad_maximum_fusion
  46.9 9.8 %all-to-all-done.1 = bf16[64,8,512]{2,1,0:T(8,128)(2,1)} async-done(((bf16[64,8,512]{2,1,0:T(8,128)(2,1)}), bf16[64,8,512]{2,1,0:T(8,128)(2,1)}, u32[]{:S(2)}, u32[]{:S(2)}) %all-to-all-start.1) | async-done | bytes 524320 | tf_op jit(solution)/shard_map/all_to_all | solution.py:177
  56.6 1.1 fusion.6
  57.8 2.9 %collective-permute-start = (bf16[256,512]{1,0:T(8,128)(2,1)S(1)}, bf16[256,512]{1,0:T(8,128)(2,1)S(1)}, u32[]{:S(2)}, u32[]{:S(2)}) collective-permute-start(bf16[256,512]{1,0:T(8,128)(2,1)S(1)} %get-tuple-element.52.refs_0_), channel_id=1, source_target_pairs={{0,64},{64,128},{128,192},{192,256},{256,320},{320,384},{384,448},... | collective-permute-start | bytes 786440 | tf_op jit(solution)/shard_map/ppermute | solution.py:134
  60.6 4.2 %collective-permute-start.4 = (bf16[256,512]{1,0:T(8,128)(2,1)S(1)}, bf16[256,512]{1,0:T(8,128)(2,1)S(1)}, u32[]{:S(2)}, u32[]{:S(2)}) collective-permute-start(bf16[256,512]{1,0:T(8,128)(2,1)S(1)} %get-tuple-element.51.refs_1_), channel_id=1, source_target_pairs={{0,448},{64,0},{128,64},{192,128},{256,192},{320,256},{384,320},{4... | collective-permute-start | bytes 786440 | tf_op jit(solution)/shard_map/ppermute | solution.py:134
  64.8 1.9 collective-permute-start.8
  66.8 3.9 %collective-permute-start.9 = (bf16[256,512]{1,0:T(8,128)(2,1)S(1)}, bf16[256,512]{1,0:T(8,128)(2,1)S(1)}, u32[]{:S(2)}, u32[]{:S(2)}) collective-permute-start(bf16[256,512]{1,0:T(8,128)(2,1)S(1)} %get-tuple-element.51.refs_1_), channel_id=1, source_target_pairs={{0,64},{64,128},{128,192},{192,256},{256,320},{320,384},{384,448},... | collective-permute-start | bytes 786440 | tf_op jit(solution)/shard_map/ppermute | solution.py:134
  70.7 1.9 collective-permute-start.1
  72.6 5.1 %collective-permute-start.5 = (bf16[256,512]{1,0:T(8,128)(2,1)S(1)}, bf16[256,512]{1,0:T(8,128)(2,1)S(1)}, u32[]{:S(2)}, u32[]{:S(2)}) collective-permute-start(bf16[256,512]{1,0:T(8,128)(2,1)S(1)} %collective-permute-done.4.refs_3_), channel_id=1, source_target_pairs={{0,448},{64,0},{128,64},{192,128},{256,192},{320,256},{384,320},{4... | collective-permute-start | bytes 786440 | tf_op jit(solution)/shard_map/ppermute | solution.py:134
  77.8 2.5 %collective-permute-start.10 = (bf16[256,512]{1,0:T(8,128)(2,1)S(1)}, bf16[256,512]{1,0:T(8,128)(2,1)S(1)}, u32[]{:S(2)}, u32[]{:S(2)}) collective-permute-start(bf16[256,512]{1,0:T(8,128)(2,1)S(1)} %collective-permute-done.8.refs_2_), channel_id=1, source_target_pairs={{0,448},{64,0},{128,64},{192,128},{256,192},{320,256},{384,320},{4... | collective-permute-start | bytes 786440 | tf_op jit(solution)/shard_map/ppermute | solution.py:134
  80.3 0.0 collective-permute-done.9.refs_5_
  80.3 3.3 %collective-permute-start.11 = (bf16[256,512]{1,0:T(8,128)(2,1)S(1)}, bf16[256,512]{1,0:T(8,128)(2,1)S(1)}, u32[]{:S(2)}, u32[]{:S(2)}) collective-permute-start(bf16[256,512]{1,0:T(8,128)(2,1)S(1)} %collective-permute-done.9.refs_5_), channel_id=1, source_target_pairs={{0,64},{64,128},{128,192},{192,256},{256,320},{320,384},{384,448},... | collective-permute-start | bytes 786440 | tf_op jit(solution)/shard_map/ppermute | solution.py:134
  83.7 0.0 collective-permute-done.1.refs_8_
  83.7 1.9 collective-permute-start.2
  85.6 5.1 %collective-permute-start.6 = (bf16[256,512]{1,0:T(8,128)(2,1)S(1)}, bf16[256,512]{1,0:T(8,128)(2,1)S(1)}, u32[]{:S(2)}, u32[]{:S(2)}) collective-permute-start(bf16[256,512]{1,0:T(8,128)(2,1)S(1)} %collective-permute-done.5.refs_7_), channel_id=1, source_target_pairs={{0,448},{64,0},{128,64},{192,128},{256,192},{320,256},{384,320},{4... | collective-permute-start | bytes 786440 | tf_op jit(solution)/shard_map/ppermute | solution.py:134
  90.7 0.0 collective-permute-done.10.refs_6_
  90.8 2.5 %collective-permute-start.12 = (bf16[256,512]{1,0:T(8,128)(2,1)S(1)}, bf16[256,512]{1,0:T(8,128)(2,1)S(1)}, u32[]{:S(2)}, u32[]{:S(2)}) collective-permute-start(bf16[256,512]{1,0:T(8,128)(2,1)S(1)} %collective-permute-done.10.refs_6_), channel_id=1, source_target_pairs={{0,448},{64,0},{128,64},{192,128},{256,192},{320,256},{384,320},{4... | collective-permute-start | bytes 786440 | tf_op jit(solution)/shard_map/ppermute | solution.py:134
  93.3 3.3 %collective-permute-start.13 = (bf16[256,512]{1,0:T(8,128)(2,1)S(1)}, bf16[256,512]{1,0:T(8,128)(2,1)S(1)}, u32[]{:S(2)}, u32[]{:S(2)}) collective-permute-start(bf16[256,512]{1,0:T(8,128)(2,1)S(1)} %collective-permute-done.11.refs_9_), channel_id=1, source_target_pairs={{0,64},{64,128},{128,192},{192,256},{256,320},{320,384},{384,448},... | collective-permute-start | bytes 786440 | tf_op jit(solution)/shard_map/ppermute | solution.py:134
  96.6 1.9 collective-permute-start.3
  98.6 0.0 collective-permute-done.6.refs_11_
  98.6 5.1 %collective-permute-start.7 = (bf16[256,512]{1,0:T(8,128)(2,1)S(1)}, bf16[256,512]{1,0:T(8,128)(2,1)S(1)}, u32[]{:S(2)}, u32[]{:S(2)}) collective-permute-start(bf16[256,512]{1,0:T(8,128)(2,1)S(1)} %collective-permute-done.6.refs_11_), channel_id=1, source_target_pairs={{0,448},{64,0},{128,64},{192,128},{256,192},{320,256},{384,320},{4... | collective-permute-start | bytes 786440 | tf_op jit(solution)/shard_map/ppermute | solution.py:134
  103.7 2.6 %shard_map.131 = (f32[512,128]{1,0:T(8,128)S(1)}, bf16[128,4096]{1,0:T(8,128)(2,1)}) custom-call(bf16[256,512]{1,0:T(8,128)(2,1)S(1)} %get-tuple-element.52.refs_0_, bf16[256,512]{1,0:T(8,128)(2,1)S(1)} %get-tuple-element.51.refs_1_, bf16[256,512]{1,0:T(8,128)(2,1)S(1)} %collective-permute-done.8.refs_2_, ...), custom_call_target="tpu_custom_call" | custom-call | flops 1073741824 | bytes 6160384 | tf_op jit(solution)/shard_map/pallas_call | solution.py:30
  106.3 0.2 collective-permute-done.3.refs_0_
  106.5 1.1 collective-permute-done.7.refs_1_
  107.6 2.5 %shard_map.132 = (bf16[8,512,512]{2,1,0:T(8,128)(2,1)}, bf16[128,512]{1,0:T(8,128)(2,1)S(1)}) custom-call(bf16[256,512]{1,0:T(8,128)(2,1)S(1)} %collective-permute-done.3.refs_0_, bf16[256,512]{1,0:T(8,128)(2,1)S(1)} %collective-permute-done.7.refs_1_, bf16[128,512]{1,0:T(8,128)(2,1)S(1)} %get-tuple-element.32.refs_14_.refs_2_, ...), custom_call_target="tpu_custom_call" | custom-call | flops 1073741824 | bytes 8912896 | tf_op jit(solution)/shard_map/pallas_call | solution.py:30
  110.1 0.0 all-gather.4.cloned.1.call-done.proj_ref
  110.2 0.0 copy-start.10
  110.2 0.0 reduce-scatter.2.cloned.1.call-update
  110.2 0.0 all-gather.6.cloned.1.call-start
  110.3 0.7 constant_dynamic-update-slice_fusion
  110.9 53.5 %reduce-scatter.2.cloned.1.call-done = bf16[512,512]{1,0:T(8,128)(2,1)} async-done(((bf16[4096,512]{1,0:T(8,128)(2,1)}), bf16[512,512]{1,0:T(8,128)(2,1)}) %reduce-scatter.2.cloned.1.call-update) | async-done | bytes 524304 | tf_op jit(solution)/shard_map/reduce_scatter | solution.py:231
  164.4 0.0 all-gather.6.cloned.1.call-update
  164.4 27.8 %all_to_all.34 = bf16[64,8,512]{2,1,0:T(8,128)(2,1)S(1)} all-to-all(bf16[64,8,512]{2,1,0:T(8,128)(2,1)} %bitcast.31), channel_id=1, replica_groups=mesh['tensor'=8,'expert'=64] {'expert'}, dimensions={0} | all-to-all | bytes 1048576 | tf_op jit(solution)/shard_map/all_to_all | solution.py:240
  192.3 0.9 shard_map.133
  193.2 4.2 %all-to-all-start.3 = ((bf16[8,32,512]{2,1,0:T(8,128)(2,1)}), bf16[8,32,512]{2,1,0:T(8,128)(2,1)S(1)}, u32[]{:S(2)}, u32[]{:S(2)}) async-start(bf16[8,32,512]{2,1,0:T(8,128)(2,1)} %shard_map.133), calls=%async_computation.4 | async-start | bytes 524288 | tf_op jit(solution)/shard_map/all_to_all | solution.py:249
  197.4 10.7 %all-gather.6.cloned.1.call-done = bf16[128,4096]{1,0:T(8,128)(2,1)} async-done(((bf16[16,4096]{1,0:T(8,128)(2,1)}), bf16[128,4096]{1,0:T(8,128)(2,1)}) %all-gather.6.cloned.1.call-update) | async-done | bytes 1048592 | tf_op jit(solution)/shard_map/all_gather | solution.py:237
  208.1 1.5 fusion.5
  209.6 0.1 reshape.85.rows_ref
  209.7 0.1 reshape.86.norm_ref
  209.8 2.2 copy-done
  211.9 1.6 shard_map.134
  (27 shorter events, 0.1 us)
Async XLA Ops:
  7.2 39.0 %copy-start.11 = (bf16[1,4,4096]{2,1,0:T(4,128)(2,1)S(1)}, bf16[1,4,4096]{2,1,0:T(4,128)(2,1)}, u32[]{:S(2)}) copy-start(bf16[1,4,4096]{2,1,0:T(4,128)(2,1)} %param.11) | copy-start | bytes 98308
  7.2 38.9 %copy-start.12 = (bf16[1,4,4096]{2,1,0:T(4,128)(2,1)S(1)}, bf16[1,4,4096]{2,1,0:T(4,128)(2,1)}, u32[]{:S(2)}) copy-start(bf16[1,4,4096]{2,1,0:T(4,128)(2,1)} %param.12) | copy-start | bytes 98308
  7.2 103.0 %all-gather.4.cloned.1.call-start = ((), (), s32[]{:S(2)}) async-start(), calls=%async_computation.5 | async-start | bytes 4259840 | tf_op jit(solution)/shard_map/all_gather | solution.py:183
  7.9 18.4 %all-to-all-start = ((bf16[4,8,512]{2,0,1:T(4,128)(2,1)}), bf16[4,8,512]{2,0,1:T(4,128)(2,1)S(1)}, u32[]{:S(2)}, u32[]{:S(2)}) async-start(bf16[4,8,512]{2,0,1:T(4,128)(2,1)} %bitcast.34), calls=%async_computation | async-start | bytes 65536 | tf_op jit(solution)/shard_map/all_to_all | solution.py:175
  27.4 29.3 %all-to-all-start.1 = ((bf16[64,8,512]{2,1,0:T(8,128)(2,1)}), bf16[64,8,512]{2,1,0:T(8,128)(2,1)}, u32[]{:S(2)}, u32[]{:S(2)}) async-start(bf16[64,8,512]{2,1,0:T(8,128)(2,1)} %fusion.1), calls=%async_computation.1 | async-start | bytes 1048576 | tf_op jit(solution)/shard_map/all_to_all | solution.py:177
  38.2 126.3 %reduce-scatter.2.cloned.1.call-start = ((), (), s32[]{:S(2)}) async-start(), calls=%async_computation.6 | async-start | bytes 4718592 | tf_op jit(solution)/shard_map/reduce_scatter | solution.py:231
  38.2 1.2 copy-start.1
  39.4 1.2 copy-start.2
  40.7 1.2 copy-start.3
  41.9 0.9 copy-start.8
  42.8 0.9 copy-start.9
  44.7 0.7 copy-start.4
  45.4 0.7 copy-start.6
  56.6 51.0 %copy-start.5 = (f32[512,128]{1,0:T(8,128)S(1)}, f32[512,128]{1,0:T(8,128)}, u32[]{:S(2)}) copy-start(f32[512,128]{1,0:T(8,128)} %copy-done.4) | copy-start | bytes 786436
  56.6 51.0 %copy-start.7 = (f32[512,128]{1,0:T(8,128)S(1)}, f32[512,128]{1,0:T(8,128)}, u32[]{:S(2)}) copy-start(f32[512,128]{1,0:T(8,128)} %copy-done.6) | copy-start | bytes 786436
  57.8 12.9 %collective-permute-start = (bf16[256,512]{1,0:T(8,128)(2,1)S(1)}, bf16[256,512]{1,0:T(8,128)(2,1)S(1)}, u32[]{:S(2)}, u32[]{:S(2)}) collective-permute-start(bf16[256,512]{1,0:T(8,128)(2,1)S(1)} %get-tuple-element.52.refs_0_), channel_id=1, source_target_pairs={{0,64},{64,128},{128,192},{192,256},{256,320},{320,384},{384,448},... | collective-permute-start | bytes 786440 | tf_op jit(solution)/shard_map/ppermute | solution.py:134
  60.6 12.0 %collective-permute-start.4 = (bf16[256,512]{1,0:T(8,128)(2,1)S(1)}, bf16[256,512]{1,0:T(8,128)(2,1)S(1)}, u32[]{:S(2)}, u32[]{:S(2)}) collective-permute-start(bf16[256,512]{1,0:T(8,128)(2,1)S(1)} %get-tuple-element.51.refs_1_), channel_id=1, source_target_pairs={{0,448},{64,0},{128,64},{192,128},{256,192},{320,256},{384,320},{4... | collective-permute-start | bytes 786440 | tf_op jit(solution)/shard_map/ppermute | solution.py:134
  64.8 13.0 %collective-permute-start.8 = (bf16[256,512]{1,0:T(8,128)(2,1)S(1)}, bf16[256,512]{1,0:T(8,128)(2,1)S(1)}, u32[]{:S(2)}, u32[]{:S(2)}) collective-permute-start(bf16[256,512]{1,0:T(8,128)(2,1)S(1)} %get-tuple-element.52.refs_0_), channel_id=1, source_target_pairs={{0,448},{64,0},{128,64},{192,128},{256,192},{320,256},{384,320},{4... | collective-permute-start | bytes 786440 | tf_op jit(solution)/shard_map/ppermute | solution.py:134
  66.8 13.6 %collective-permute-start.9 = (bf16[256,512]{1,0:T(8,128)(2,1)S(1)}, bf16[256,512]{1,0:T(8,128)(2,1)S(1)}, u32[]{:S(2)}, u32[]{:S(2)}) collective-permute-start(bf16[256,512]{1,0:T(8,128)(2,1)S(1)} %get-tuple-element.51.refs_1_), channel_id=1, source_target_pairs={{0,64},{64,128},{128,192},{192,256},{256,320},{320,384},{384,448},... | collective-permute-start | bytes 786440 | tf_op jit(solution)/shard_map/ppermute | solution.py:134
  70.7 13.0 %collective-permute-start.1 = (bf16[256,512]{1,0:T(8,128)(2,1)S(1)}, bf16[256,512]{1,0:T(8,128)(2,1)S(1)}, u32[]{:S(2)}, u32[]{:S(2)}) collective-permute-start(bf16[256,512]{1,0:T(8,128)(2,1)S(1)} %collective-permute-done.refs_4_), channel_id=1, source_target_pairs={{0,64},{64,128},{128,192},{192,256},{256,320},{320,384},{384,448},... | collective-permute-start | bytes 786440 | tf_op jit(solution)/shard_map/ppermute | solution.py:134
  72.6 13.0 %collective-permute-start.5 = (bf16[256,512]{1,0:T(8,128)(2,1)S(1)}, bf16[256,512]{1,0:T(8,128)(2,1)S(1)}, u32[]{:S(2)}, u32[]{:S(2)}) collective-permute-start(bf16[256,512]{1,0:T(8,128)(2,1)S(1)} %collective-permute-done.4.refs_3_), channel_id=1, source_target_pairs={{0,448},{64,0},{128,64},{192,128},{256,192},{320,256},{384,320},{4... | collective-permute-start | bytes 786440 | tf_op jit(solution)/shard_map/ppermute | solution.py:134
  77.8 13.0 %collective-permute-start.10 = (bf16[256,512]{1,0:T(8,128)(2,1)S(1)}, bf16[256,512]{1,0:T(8,128)(2,1)S(1)}, u32[]{:S(2)}, u32[]{:S(2)}) collective-permute-start(bf16[256,512]{1,0:T(8,128)(2,1)S(1)} %collective-permute-done.8.refs_2_), channel_id=1, source_target_pairs={{0,448},{64,0},{128,64},{192,128},{256,192},{320,256},{384,320},{4... | collective-permute-start | bytes 786440 | tf_op jit(solution)/shard_map/ppermute | solution.py:134
  80.3 13.0 %collective-permute-start.11 = (bf16[256,512]{1,0:T(8,128)(2,1)S(1)}, bf16[256,512]{1,0:T(8,128)(2,1)S(1)}, u32[]{:S(2)}, u32[]{:S(2)}) collective-permute-start(bf16[256,512]{1,0:T(8,128)(2,1)S(1)} %collective-permute-done.9.refs_5_), channel_id=1, source_target_pairs={{0,64},{64,128},{128,192},{192,256},{256,320},{320,384},{384,448},... | collective-permute-start | bytes 786440 | tf_op jit(solution)/shard_map/ppermute | solution.py:134
  83.7 13.0 %collective-permute-start.2 = (bf16[256,512]{1,0:T(8,128)(2,1)S(1)}, bf16[256,512]{1,0:T(8,128)(2,1)S(1)}, u32[]{:S(2)}, u32[]{:S(2)}) collective-permute-start(bf16[256,512]{1,0:T(8,128)(2,1)S(1)} %collective-permute-done.1.refs_8_), channel_id=1, source_target_pairs={{0,64},{64,128},{128,192},{192,256},{256,320},{320,384},{384,448},... | collective-permute-start | bytes 786440 | tf_op jit(solution)/shard_map/ppermute | solution.py:134
  85.6 13.0 %collective-permute-start.6 = (bf16[256,512]{1,0:T(8,128)(2,1)S(1)}, bf16[256,512]{1,0:T(8,128)(2,1)S(1)}, u32[]{:S(2)}, u32[]{:S(2)}) collective-permute-start(bf16[256,512]{1,0:T(8,128)(2,1)S(1)} %collective-permute-done.5.refs_7_), channel_id=1, source_target_pairs={{0,448},{64,0},{128,64},{192,128},{256,192},{320,256},{384,320},{4... | collective-permute-start | bytes 786440 | tf_op jit(solution)/shard_map/ppermute | solution.py:134
  90.8 13.0 %collective-permute-start.12 = (bf16[256,512]{1,0:T(8,128)(2,1)S(1)}, bf16[256,512]{1,0:T(8,128)(2,1)S(1)}, u32[]{:S(2)}, u32[]{:S(2)}) collective-permute-start(bf16[256,512]{1,0:T(8,128)(2,1)S(1)} %collective-permute-done.10.refs_6_), channel_id=1, source_target_pairs={{0,448},{64,0},{128,64},{192,128},{256,192},{320,256},{384,320},{4... | collective-permute-start | bytes 786440 | tf_op jit(solution)/shard_map/ppermute | solution.py:134
  93.3 10.4 %collective-permute-start.13 = (bf16[256,512]{1,0:T(8,128)(2,1)S(1)}, bf16[256,512]{1,0:T(8,128)(2,1)S(1)}, u32[]{:S(2)}, u32[]{:S(2)}) collective-permute-start(bf16[256,512]{1,0:T(8,128)(2,1)S(1)} %collective-permute-done.11.refs_9_), channel_id=1, source_target_pairs={{0,64},{64,128},{128,192},{192,256},{256,320},{320,384},{384,448},... | collective-permute-start | bytes 786440 | tf_op jit(solution)/shard_map/ppermute | solution.py:134
  96.6 9.9 %collective-permute-start.3 = (bf16[256,512]{1,0:T(8,128)(2,1)S(1)}, bf16[256,512]{1,0:T(8,128)(2,1)S(1)}, u32[]{:S(2)}, u32[]{:S(2)}) collective-permute-start(bf16[256,512]{1,0:T(8,128)(2,1)S(1)} %collective-permute-done.2.refs_12_), channel_id=1, source_target_pairs={{0,64},{64,128},{128,192},{192,256},{256,320},{320,384},{384,448},... | collective-permute-start | bytes 786440 | tf_op jit(solution)/shard_map/ppermute | solution.py:134
  98.6 9.0 %collective-permute-start.7 = (bf16[256,512]{1,0:T(8,128)(2,1)S(1)}, bf16[256,512]{1,0:T(8,128)(2,1)S(1)}, u32[]{:S(2)}, u32[]{:S(2)}) collective-permute-start(bf16[256,512]{1,0:T(8,128)(2,1)S(1)} %collective-permute-done.6.refs_11_), channel_id=1, source_target_pairs={{0,448},{64,0},{128,64},{192,128},{256,192},{320,256},{384,320},{4... | collective-permute-start | bytes 786440 | tf_op jit(solution)/shard_map/ppermute | solution.py:134
  110.2 99.6 %copy-start.10 = (f32[4096]{0:T(1024)S(1)}, f32[4096]{0:T(1024)}, u32[]{:S(2)}) copy-start(f32[4096]{0:T(1024)} %param.13) | copy-start | bytes 49156
  110.2 97.9 %all-gather.6.cloned.1.call-start = ((), (), s32[]{:S(2)}) async-start(), calls=%async_computation.7 | async-start | bytes 1179648 | tf_op jit(solution)/shard_map/all_gather | solution.py:237
  193.2 16.6 %all-to-all-start.3 = ((bf16[8,32,512]{2,1,0:T(8,128)(2,1)}), bf16[8,32,512]{2,1,0:T(8,128)(2,1)S(1)}, u32[]{:S(2)}, u32[]{:S(2)}) async-start(bf16[8,32,512]{2,1,0:T(8,128)(2,1)} %shard_map.133), calls=%async_computation.4 | async-start | bytes 524288 | tf_op jit(solution)/shard_map/all_to_all | solution.py:249
  209.8 2.2 copy-start
Sparse Core Ops, SparseCore 0:
  11.4 88.2 all-gather.3
  110.3 54.0 reduce-scatter.1
  166.5 41.5 all-gather.5

commit v3 on v2

--- a/solution.py
+++ b/solution.py
@@ -25,15 +25,15 @@
     return [pl.BlockSpec(memory_space=pltpu.VMEM)] * count
 
 
-def call(kernel, out_shapes, args, flops, scratch=(), out_specs=None):
+def call(kernel, out_shapes, args, flops, scratch=(), out_specs=None, in_specs=None, limit=VMEM_BYTES):
     moved = sum(math.prod(a.shape) * a.dtype.itemsize for a in (*args, *out_shapes))
     return pl.pallas_call(
         kernel,
         out_shape=list(out_shapes),
-        in_specs=vmem_specs(len(args)),
+        in_specs=in_specs or vmem_specs(len(args)),
         out_specs=out_specs or vmem_specs(len(out_shapes)),
         scratch_shapes=list(scratch),
-        compiler_params=pltpu.CompilerParams(vmem_limit_bytes=VMEM_BYTES),
+        compiler_params=pltpu.CompilerParams(vmem_limit_bytes=limit),
         cost_estimate=pl.CostEstimate(flops=flops, bytes_accessed=moved, transcendentals=0),
     )(*args)
 
@@ -82,7 +82,7 @@
 
 def late_kernel(width, *refs):
     chunks, (hidden, total_ref, slope_ref, act_ref, down_ref, side_ref) = refs[:2], refs[2:8]
-    part_hbm, out, grads_ref, part_ref, sems = refs[8:]
+    part_hbm, out_hbm, grads_ref, part_ref, down_part, sems = refs[8:]
     rows = chunks[0].shape[0]
     hid = slope_ref.shape[1]
     cols = slice_at(OFFSETS[7], width)
@@ -101,7 +101,9 @@
         copies[-1].start()
     down = dot(hidden[:, :rows], chunks[0][...], PLAIN)
     down = down + dot(hidden[:, rows:], chunks[1][...], PLAIN)
-    out[...] = down.astype(BF16)
+    down_part[...] = down.astype(BF16)
+    copies.append(pltpu.make_async_copy(down_part, out_hbm, sems.at[len(copies)]))
+    copies[-1].start()
     for copy in copies:
         copy.wait()
 
@@ -112,20 +114,53 @@
         out_ref[j] = total
 
 
-def tail_kernel(moe_ref, rows_ref, norm_ref, gain_ref, proj_ref, resid_ref, attn_ref, held):
+def tail_kernel(
+    moe_hbm,
+    every_hbm,
+    gain_hbm,
+    proj_hbm,
+    resid_ref,
+    attn_ref,
+    moe_ref,
+    every_ref,
+    gain_ref,
+    proj_ref,
+    rows_ref,
+    norm_ref,
+    sems,
+):
     n, _, width = moe_ref.shape
     model = n * width
-    norm_in = norm_ref[...].astype(F32)
+    own = resid_ref.shape[0]
+    pieces = [pl.ds(j * width, width) for j in range(n)]
+    pairs = [(every_hbm, every_ref), (moe_hbm, moe_ref), (gain_hbm, gain_ref)]
+    pairs += [(proj_hbm.at[piece], proj_ref.at[piece]) for piece in pieces]
+    copies = [pltpu.make_async_copy(a, b, sems.at[i]) for i, (a, b) in enumerate(pairs)]
+    for copy in copies:
+        copy.start()
+    copies[0].wait()
+    for j in range(n):
+        both = every_ref[j].astype(F32)
+        rows_ref[pl.ds(j * own, own), :] = both[:own]
+        norm_ref[pl.ds(j * own, own), :] = both[own : 2 * own]
+    norm_in = norm_ref[...]
     inv = lax.rsqrt(jnp.sum(norm_in * norm_in, axis=-1, keepdims=True) / model + 1e-06)
+    copies[1].wait()
+    copies[2].wait()
     moe = jnp.concatenate([moe_ref[j] for j in range(n)], axis=1).astype(F32)
     scaled = gain_ref[...] * moe
     along = jnp.sum(scaled * norm_in, axis=-1, keepdims=True)
-    resid = rows_ref[...].astype(F32) + inv * scaled - inv * inv * inv / model * norm_in * along
-    held[...] = resid
-    attn_ref[...] = dot(resid.astype(BF16), proj_ref[...], PLAIN).astype(BF16)
-    own = resid_ref.shape[0]
+    rows_ref[...] = (
+        rows_ref[...] + inv * scaled - inv * inv * inv / model * norm_in * along
+    )
+    total = None
+    for j, piece in enumerate(pieces):
+        copies[3 + j].wait()
+        term = dot(rows_ref[:, piece].astype(BF16), proj_ref[piece, :], PLAIN)
+        total = term if total is None else total + term
+    attn_ref[...] = total.astype(BF16)
     index = lax.axis_index("tensor")
-    pair = held[pl.ds(pl.multiple_of(index // 2 * 2 * own, 2 * own), 2 * own), :]
+    pair = rows_ref[pl.ds(pl.multiple_of(index // 2 * 2 * own, 2 * own), 2 * own), :]
     resid_ref[...] = jnp.where(lax.rem(index, 2) == 0, pair[:own], pair[own:]).astype(BF16)
 
 
@@ -217,15 +252,16 @@
     )
     part, last_down = call(
         functools.partial(late_kernel, width),
-        (pltpu.HBM((n, slots, width), BF16), struct((hid, width), BF16)),
+        (pltpu.HBM((n, slots, width), BF16), pltpu.HBM((hid, width), BF16)),
         (*chunks[14:], hidden, total, slope, act, down_t, side_t),
         4 * slots * model * hid,
         (
             pltpu.VMEM((slots, 2 * hid), BF16),
             pltpu.VMEM((n, slots, width), BF16),
-            pltpu.SemaphoreType.DMA((n,)),
+            pltpu.VMEM((hid, width), BF16),
+            pltpu.SemaphoreType.DMA((n + 1,)),
         ),
-        [pl.BlockSpec(memory_space=pltpu.HBM), *vmem_specs(1)],
+        [pl.BlockSpec(memory_space=pltpu.HBM)] * 2,
     )
     part, proj = lax.optimization_barrier((part, proj))
     sums = lax.psum_scatter(
@@ -235,8 +271,6 @@
     down_grad = lax.dynamic_update_slice(down_grad, last_down, (0, last))
     sums, both, down_grad = lax.optimization_barrier((sums, both, down_grad))
     every = lax.all_gather(both, "tensor", axis=0)
-    all_rows = every[:, :own].reshape(tokens, model)
-    all_norm = every[:, own : 2 * own].reshape(tokens, model)
     returned = lax.all_to_all(
         sums.reshape(experts, cap, width), "expert", 0, 0, tiled=True
     ).reshape(slots, width)
@@ -250,9 +284,19 @@
     resid_grad, attn_grad = call(
         tail_kernel,
         (struct((own, model), BF16), struct((tokens, out_proj.shape[0]), BF16)),
-        (moe, all_rows, all_norm, norm_gain[None], proj),
+        (moe, every, norm_gain[None], proj),
         2 * tokens * model * out_proj.shape[0],
-        (pltpu.VMEM((tokens, model), F32),),
+        (
+            pltpu.VMEM(moe.shape, BF16),
+            pltpu.VMEM(every.shape, BF16),
+            pltpu.VMEM((1, model), F32),
+            pltpu.VMEM(proj.shape, BF16),
+            pltpu.VMEM((tokens, model), F32),
+            pltpu.VMEM((tokens, model), F32),
+            pltpu.SemaphoreType.DMA((3 + n,)),
+        ),
+        in_specs=[pl.BlockSpec(memory_space=pltpu.HBM)] * 4,
+        limit=60 * 1024 * 1024,
     )
     return (resid_grad[None], attn_grad[None], down_grad[None])
 

time: 222 us -> 221 us (level)
  blocking collectives: 27.8 us -> 43.4 us
  waiting for transfers between devices: 81.7 us -> 70.2 us
  starting transfers between devices: 71.1 us -> 67 us
  local copies, waits for them, and re-layouts: 14.3 us -> 11.2 us
    all_to_all x0 -> x1, blocking collectives: none -> 15.5 us  [per_device(): moe = lax.all_to_all(own_moe, 'tensor', 0, 0, tiled=True)]
    all_gather x1, waiting for transfers between devices: 10.7 us -> 0.01 us  [per_device(): every = lax.all_gather(both, 'tensor', axis=0)]
    all_to_all x1 -> x0, starting transfers between devices: 4.18 us -> none  [per_device(): moe = lax.all_to_all(own_moe, 'tensor', 0, 0, tiled=True)]
    unnamed x28 -> x26, local copies, waits for them, and re-layouts: 10.6 us -> 9.2 us
  transfers between devices with their start and end apart: 20 -> 19, of which waited for: 6 -> 5; matrix products, arithmetic and copies ran while one was open for 3% -> 3% of each run, Pallas kernels for 3% -> 3%
where the time goes in v3:
time: 221 us; the launch traced here: 218 us
  waiting for transfers between devices  70.2 us (32%)
  starting transfers between devices  67 us (30%)
  blocking collectives  43.4 us (20%)
  between operations  14.1 us (6%)
  local copies, waits for them, and re-layouts  11.2 us (5%)
  Pallas kernels  9.82 us (4%)
    reduce_scatter x1, waiting for transfers between devices, per_device(): lax.psum_scatter(part.reshape(n * slots, width), 'tensor', scatter_dimens...  52.7 us
    ppermute x14, starting transfers between devices, shift(): return lax.ppermute(x, 'tensor', [(i, (i + step) % n) for i in range(n)])  45.7 us
    all_to_all x1, blocking collectives, per_device(): lax.all_to_all(sums.reshape(experts, cap, width), 'expert', 0, 0, tiled=T...  27.8 us
    all_to_all x1, blocking collectives, per_device(): moe = lax.all_to_all(own_moe, 'tensor', 0, 0, tiled=True)  15.5 us
    all_to_all x1, starting transfers between devices, per_device(): lax.all_to_all(scaled.reshape(experts, cap, width), 'expert', 0, 0, tiled...  10.8 us
    all_to_all x1, starting transfers between devices, per_device(): own_rows = lax.all_to_all(out_grad[0], 'tensor', 1, 0, tiled=True)  10.3 us
    all_to_all x1, waiting for transfers between devices, per_device(): lax.all_to_all(scaled.reshape(experts, cap, width), 'expert', 0, 0, tiled...  9.83 us
    pallas_call x5, Pallas kernels, call(): pl.pallas_call(kernel, out_shape=list(out_shapes), in_specs=in_specs or v...  9.82 us
  transfers between devices with their start and end apart: 19, of which 5 were waited for; matrix products, arithmetic and copies ran while one was open for 3% of the time, Pallas kernels for 3%

profile of v3, /device:TPU:6, one launch (start us, length us, event | category | flops | bytes accessed | tf_op | source)
XLA Modules:
  0.0 218.1 jit_solution(16752668709409307762)
XLA Ops:
  7.2 0.0 all-gather.4.cloned.1.call-start
  7.2 0.7 all-gather.4.cloned.1.call-update
  7.9 10.3 %all-to-all-start = ((bf16[4,8,512]{2,0,1:T(4,128)(2,1)}), bf16[4,8,512]{2,0,1:T(4,128)(2,1)S(1)}, u32[]{:S(2)}, u32[]{:S(2)}) async-start(bf16[4,8,512]{2,0,1:T(4,128)(2,1)} %bitcast.33), calls=%async_computation | async-start | bytes 65536 | tf_op jit(solution)/shard_map/all_to_all | solution.py:210
  18.2 0.8 copy.19
  19.0 0.1 reshape_squeeze.4
  19.1 0.8 copy.21
  19.9 0.1 broadcast_in_dim.33
  20.0 0.2 convert_reduce_fusion
  20.1 0.3 convolution_convert_fusion.pick_ref
  20.5 0.2 select_reduce_fusion
  20.6 5.7 %all-to-all-done = bf16[4,8,512]{2,0,1:T(4,128)(2,1)S(1)} async-done(((bf16[4,8,512]{2,0,1:T(4,128)(2,1)}), bf16[4,8,512]{2,0,1:T(4,128)(2,1)S(1)}, u32[]{:S(2)}, u32[]{:S(2)}) %all-to-all-start) | async-done | bytes 32800 | tf_op jit(solution)/shard_map/all_to_all | solution.py:210
  26.3 1.1 fusion.1
  27.4 10.8 %all-to-all-start.1 = ((bf16[64,8,512]{2,1,0:T(8,128)(2,1)}), bf16[64,8,512]{2,1,0:T(8,128)(2,1)}, u32[]{:S(2)}, u32[]{:S(2)}) async-start(bf16[64,8,512]{2,1,0:T(8,128)(2,1)} %fusion.1), calls=%async_computation.1 | async-start | bytes 1048576 | tf_op jit(solution)/shard_map/all_to_all | solution.py:212
  38.2 0.0 reduce-scatter.2.cloned.1.call-start
  38.2 0.0 copy-start
  38.2 1.2 copy-done
  39.4 1.2 copy-done.1
  40.7 1.2 copy-done.2
  41.9 0.9 copy-done.7
  42.8 0.9 copy-done.8
  43.7 1.0 shard_map.130
  44.7 0.7 copy-done.3
  45.4 0.7 copy-done.5
  46.1 0.7 pad_maximum_fusion
  46.8 9.8 %all-to-all-done.1 = bf16[64,8,512]{2,1,0:T(8,128)(2,1)} async-done(((bf16[64,8,512]{2,1,0:T(8,128)(2,1)}), bf16[64,8,512]{2,1,0:T(8,128)(2,1)}, u32[]{:S(2)}, u32[]{:S(2)}) %all-to-all-start.1) | async-done | bytes 524320 | tf_op jit(solution)/shard_map/all_to_all | solution.py:212
  56.6 1.1 fusion.5
  57.8 2.9 %collective-permute-start = (bf16[256,512]{1,0:T(8,128)(2,1)S(1)}, bf16[256,512]{1,0:T(8,128)(2,1)S(1)}, u32[]{:S(2)}, u32[]{:S(2)}) collective-permute-start(bf16[256,512]{1,0:T(8,128)(2,1)S(1)} %get-tuple-element.50.refs_0_), channel_id=1, source_target_pairs={{0,64},{64,128},{128,192},{192,256},{256,320},{320,384},{384,448},... | collective-permute-start | bytes 786440 | tf_op jit(solution)/shard_map/ppermute | solution.py:169
  60.6 4.2 %collective-permute-start.4 = (bf16[256,512]{1,0:T(8,128)(2,1)S(1)}, bf16[256,512]{1,0:T(8,128)(2,1)S(1)}, u32[]{:S(2)}, u32[]{:S(2)}) collective-permute-start(bf16[256,512]{1,0:T(8,128)(2,1)S(1)} %get-tuple-element.49.refs_1_), channel_id=1, source_target_pairs={{0,448},{64,0},{128,64},{192,128},{256,192},{320,256},{384,320},{4... | collective-permute-start | bytes 786440 | tf_op jit(solution)/shard_map/ppermute | solution.py:169
  64.8 1.9 collective-permute-start.8
  66.8 3.9 %collective-permute-start.9 = (bf16[256,512]{1,0:T(8,128)(2,1)S(1)}, bf16[256,512]{1,0:T(8,128)(2,1)S(1)}, u32[]{:S(2)}, u32[]{:S(2)}) collective-permute-start(bf16[256,512]{1,0:T(8,128)(2,1)S(1)} %get-tuple-element.49.refs_1_), channel_id=1, source_target_pairs={{0,64},{64,128},{128,192},{192,256},{256,320},{320,384},{384,448},... | collective-permute-start | bytes 786440 | tf_op jit(solution)/shard_map/ppermute | solution.py:169
  70.7 0.0 collective-permute-done.refs_4_
  70.7 1.9 collective-permute-start.1
  72.6 0.0 collective-permute-done.4.refs_3_
  72.6 5.1 %collective-permute-start.5 = (bf16[256,512]{1,0:T(8,128)(2,1)S(1)}, bf16[256,512]{1,0:T(8,128)(2,1)S(1)}, u32[]{:S(2)}, u32[]{:S(2)}) collective-permute-start(bf16[256,512]{1,0:T(8,128)(2,1)S(1)} %collective-permute-done.4.refs_3_), channel_id=1, source_target_pairs={{0,448},{64,0},{128,64},{192,128},{256,192},{320,256},{384,320},{4... | collective-permute-start | bytes 786440 | tf_op jit(solution)/shard_map/ppermute | solution.py:169
  77.8 0.0 collective-permute-done.8.refs_2_
  77.8 2.5 %collective-permute-start.10 = (bf16[256,512]{1,0:T(8,128)(2,1)S(1)}, bf16[256,512]{1,0:T(8,128)(2,1)S(1)}, u32[]{:S(2)}, u32[]{:S(2)}) collective-permute-start(bf16[256,512]{1,0:T(8,128)(2,1)S(1)} %collective-permute-done.8.refs_2_), channel_id=1, source_target_pairs={{0,448},{64,0},{128,64},{192,128},{256,192},{320,256},{384,320},{4... | collective-permute-start | bytes 786440 | tf_op jit(solution)/shard_map/ppermute | solution.py:169
  80.3 0.0 collective-permute-done.9.refs_5_
  80.3 3.3 %collective-permute-start.11 = (bf16[256,512]{1,0:T(8,128)(2,1)S(1)}, bf16[256,512]{1,0:T(8,128)(2,1)S(1)}, u32[]{:S(2)}, u32[]{:S(2)}) collective-permute-start(bf16[256,512]{1,0:T(8,128)(2,1)S(1)} %collective-permute-done.9.refs_5_), channel_id=1, source_target_pairs={{0,64},{64,128},{128,192},{192,256},{256,320},{320,384},{384,448},... | collective-permute-start | bytes 786440 | tf_op jit(solution)/shard_map/ppermute | solution.py:169
  83.7 0.0 collective-permute-done.1.refs_8_
  83.7 1.9 collective-permute-start.2
  85.6 0.0 collective-permute-done.5.refs_7_
  85.6 5.1 %collective-permute-start.6 = (bf16[256,512]{1,0:T(8,128)(2,1)S(1)}, bf16[256,512]{1,0:T(8,128)(2,1)S(1)}, u32[]{:S(2)}, u32[]{:S(2)}) collective-permute-start(bf16[256,512]{1,0:T(8,128)(2,1)S(1)} %collective-permute-done.5.refs_7_), channel_id=1, source_target_pairs={{0,448},{64,0},{128,64},{192,128},{256,192},{320,256},{384,320},{4... | collective-permute-start | bytes 786440 | tf_op jit(solution)/shard_map/ppermute | solution.py:169
  90.7 0.0 collective-permute-done.10.refs_6_
  90.8 2.5 %collective-permute-start.12 = (bf16[256,512]{1,0:T(8,128)(2,1)S(1)}, bf16[256,512]{1,0:T(8,128)(2,1)S(1)}, u32[]{:S(2)}, u32[]{:S(2)}) collective-permute-start(bf16[256,512]{1,0:T(8,128)(2,1)S(1)} %collective-permute-done.10.refs_6_), channel_id=1, source_target_pairs={{0,448},{64,0},{128,64},{192,128},{256,192},{320,256},{384,320},{4... | collective-permute-start | bytes 786440 | tf_op jit(solution)/shard_map/ppermute | solution.py:169
  93.3 0.0 collective-permute-done.11.refs_9_
  93.3 3.3 %collective-permute-start.13 = (bf16[256,512]{1,0:T(8,128)(2,1)S(1)}, bf16[256,512]{1,0:T(8,128)(2,1)S(1)}, u32[]{:S(2)}, u32[]{:S(2)}) collective-permute-start(bf16[256,512]{1,0:T(8,128)(2,1)S(1)} %collective-permute-done.11.refs_9_), channel_id=1, source_target_pairs={{0,64},{64,128},{128,192},{192,256},{256,320},{320,384},{384,448},... | collective-permute-start | bytes 786440 | tf_op jit(solution)/shard_map/ppermute | solution.py:169
  96.6 0.0 collective-permute-done.2.refs_12_
  96.6 1.9 collective-permute-start.3
  98.6 5.1 %collective-permute-start.7 = (bf16[256,512]{1,0:T(8,128)(2,1)S(1)}, bf16[256,512]{1,0:T(8,128)(2,1)S(1)}, u32[]{:S(2)}, u32[]{:S(2)}) collective-permute-start(bf16[256,512]{1,0:T(8,128)(2,1)S(1)} %collective-permute-done.6.refs_11_), channel_id=1, source_target_pairs={{0,448},{64,0},{128,64},{192,128},{256,192},{320,256},{384,320},{4... | collective-permute-start | bytes 786440 | tf_op jit(solution)/shard_map/ppermute | solution.py:169
  103.7 2.6 %shard_map.131 = (f32[512,128]{1,0:T(8,128)S(1)}, bf16[128,4096]{1,0:T(8,128)(2,1)}) custom-call(bf16[256,512]{1,0:T(8,128)(2,1)S(1)} %get-tuple-element.50.refs_0_, bf16[256,512]{1,0:T(8,128)(2,1)S(1)} %get-tuple-element.49.refs_1_, bf16[256,512]{1,0:T(8,128)(2,1)S(1)} %collective-permute-done.8.refs_2_, ...), custom_call_target="tpu_custom_call" | custom-call | flops 1073741824 | bytes 6160384 | tf_op jit(solution)/shard_map/pallas_call | solution.py:30
  106.3 0.2 collective-permute-done.3.refs_0_
  106.5 1.1 collective-permute-done.7.refs_1_
  107.6 2.6 %shard_map.132 = (bf16[8,512,512]{2,1,0:T(8,128)(2,1)}, bf16[128,512]{1,0:T(8,128)(2,1)}) custom-call(bf16[256,512]{1,0:T(8,128)(2,1)S(1)} %collective-permute-done.3.refs_0_, bf16[256,512]{1,0:T(8,128)(2,1)S(1)} %collective-permute-done.7.refs_1_, bf16[128,512]{1,0:T(8,128)(2,1)S(1)} %get-tuple-element.32.refs_14_.refs_2_, ...), custom_call_target="tpu_custom_call" | custom-call | flops 1073741824 | bytes 8912896 | tf_op jit(solution)/shard_map/pallas_call | solution.py:30
  110.2 0.0 all-gather.4.cloned.1.call-done.proj_hbm
  110.2 0.0 reduce-scatter.2.cloned.1.call-update
  110.2 0.0 all-gather.6.cloned.1.call-start
  110.3 0.8 copy-done.9
  111.1 0.7 constant_dynamic-update-slice_fusion
  111.8 52.7 %reduce-scatter.2.cloned.1.call-done = bf16[512,512]{1,0:T(8,128)(2,1)} async-done(((bf16[4096,512]{1,0:T(8,128)(2,1)}), bf16[512,512]{1,0:T(8,128)(2,1)}) %reduce-scatter.2.cloned.1.call-update) | async-done | bytes 524304 | tf_op jit(solution)/shard_map/reduce_scatter | solution.py:267
  164.4 0.0 all-gather.6.cloned.1.call-update
  164.5 27.8 %all_to_all.34 = bf16[64,8,512]{2,1,0:T(8,128)(2,1)S(1)} all-to-all(bf16[64,8,512]{2,1,0:T(8,128)(2,1)} %bitcast.31), channel_id=1, replica_groups=mesh['tensor'=8,'expert'=64] {'expert'}, dimensions={0} | all-to-all | bytes 1048576 | tf_op jit(solution)/shard_map/all_to_all | solution.py:274
  192.3 0.2 shard_map.133
  192.5 15.5 %all_to_all.35.moe_hbm = bf16[8,32,512]{2,1,0:T(8,128)(2,1)} all-to-all(bf16[8,32,512]{2,1,0:T(8,128)(2,1)S(1)} %shard_map.133), channel_id=1, replica_groups=mesh['tensor'=8,'expert'=64] {'tensor'}, dimensions={0} | all-to-all | bytes 524288 | tf_op jit(solution)/shard_map/all_to_all | solution.py:283
  208.1 3.5 %shard_map.134 = (bf16[4,4096]{1,0:T(4,128)(2,1)}, bf16[32,512]{1,0:T(8,128)(2,1)}) custom-call(bf16[8,32,512]{2,1,0:T(8,128)(2,1)} %all_to_all.35.moe_hbm, bf16[8,16,4096]{2,1,0:T(8,128)(2,1)} %bitcast.30, f32[1,4096]{1,0:T(1,128)} %bitcast.37, bf16[4096,512]{1,0:T(8,128)(2,1)} %all-gather.4.cloned.1.call-done.proj_hbm), custom_call_target="tpu_custom_call" | custom-call | flops 134217728 | bytes 5586944 | tf_op jit(solution)/shard_map/pallas_call | solution.py:30
  (21 shorter events, 0.1 us)
Async XLA Ops:
  7.2 38.9 %copy-start.10 = (bf16[1,4,4096]{2,1,0:T(4,128)(2,1)S(1)}, bf16[1,4,4096]{2,1,0:T(4,128)(2,1)}, u32[]{:S(2)}) copy-start(bf16[1,4,4096]{2,1,0:T(4,128)(2,1)} %param.11) | copy-start | bytes 98308
  7.2 38.9 %copy-start.11 = (bf16[1,4,4096]{2,1,0:T(4,128)(2,1)S(1)}, bf16[1,4,4096]{2,1,0:T(4,128)(2,1)}, u32[]{:S(2)}) copy-start(bf16[1,4,4096]{2,1,0:T(4,128)(2,1)} %param.12) | copy-start | bytes 98308
  7.2 103.0 %all-gather.4.cloned.1.call-start = ((), (), s32[]{:S(2)}) async-start(), calls=%async_computation.5 | async-start | bytes 4259840 | tf_op jit(solution)/shard_map/all_gather | solution.py:218
  7.9 18.4 %all-to-all-start = ((bf16[4,8,512]{2,0,1:T(4,128)(2,1)}), bf16[4,8,512]{2,0,1:T(4,128)(2,1)S(1)}, u32[]{:S(2)}, u32[]{:S(2)}) async-start(bf16[4,8,512]{2,0,1:T(4,128)(2,1)} %bitcast.33), calls=%async_computation | async-start | bytes 65536 | tf_op jit(solution)/shard_map/all_to_all | solution.py:210
  27.4 29.3 %all-to-all-start.1 = ((bf16[64,8,512]{2,1,0:T(8,128)(2,1)}), bf16[64,8,512]{2,1,0:T(8,128)(2,1)}, u32[]{:S(2)}, u32[]{:S(2)}) async-start(bf16[64,8,512]{2,1,0:T(8,128)(2,1)} %fusion.1), calls=%async_computation.1 | async-start | bytes 1048576 | tf_op jit(solution)/shard_map/all_to_all | solution.py:212
  38.2 126.3 %reduce-scatter.2.cloned.1.call-start = ((), (), s32[]{:S(2)}) async-start(), calls=%async_computation.6 | async-start | bytes 4718592 | tf_op jit(solution)/shard_map/reduce_scatter | solution.py:267
  38.2 1.2 copy-start
  39.4 1.2 copy-start.1
  40.7 1.2 copy-start.2
  41.9 0.9 copy-start.7
  42.8 0.9 copy-start.8
  44.7 0.7 copy-start.3
  45.4 0.7 copy-start.5
  56.6 51.0 %copy-start.4 = (f32[512,128]{1,0:T(8,128)S(1)}, f32[512,128]{1,0:T(8,128)}, u32[]{:S(2)}) copy-start(f32[512,128]{1,0:T(8,128)} %copy-done.3) | copy-start | bytes 786436
  56.6 51.0 %copy-start.6 = (f32[512,128]{1,0:T(8,128)S(1)}, f32[512,128]{1,0:T(8,128)}, u32[]{:S(2)}) copy-start(f32[512,128]{1,0:T(8,128)} %copy-done.5) | copy-start | bytes 786436
  57.8 12.9 %collective-permute-start = (bf16[256,512]{1,0:T(8,128)(2,1)S(1)}, bf16[256,512]{1,0:T(8,128)(2,1)S(1)}, u32[]{:S(2)}, u32[]{:S(2)}) collective-permute-start(bf16[256,512]{1,0:T(8,128)(2,1)S(1)} %get-tuple-element.50.refs_0_), channel_id=1, source_target_pairs={{0,64},{64,128},{128,192},{192,256},{256,320},{320,384},{384,448},... | collective-permute-start | bytes 786440 | tf_op jit(solution)/shard_map/ppermute | solution.py:169
  60.6 12.0 %collective-permute-start.4 = (bf16[256,512]{1,0:T(8,128)(2,1)S(1)}, bf16[256,512]{1,0:T(8,128)(2,1)S(1)}, u32[]{:S(2)}, u32[]{:S(2)}) collective-permute-start(bf16[256,512]{1,0:T(8,128)(2,1)S(1)} %get-tuple-element.49.refs_1_), channel_id=1, source_target_pairs={{0,448},{64,0},{128,64},{192,128},{256,192},{320,256},{384,320},{4... | collective-permute-start | bytes 786440 | tf_op jit(solution)/shard_map/ppermute | solution.py:169
  64.8 13.0 %collective-permute-start.8 = (bf16[256,512]{1,0:T(8,128)(2,1)S(1)}, bf16[256,512]{1,0:T(8,128)(2,1)S(1)}, u32[]{:S(2)}, u32[]{:S(2)}) collective-permute-start(bf16[256,512]{1,0:T(8,128)(2,1)S(1)} %get-tuple-element.50.refs_0_), channel_id=1, source_target_pairs={{0,448},{64,0},{128,64},{192,128},{256,192},{320,256},{384,320},{4... | collective-permute-start | bytes 786440 | tf_op jit(solution)/shard_map/ppermute | solution.py:169
  66.8 13.6 %collective-permute-start.9 = (bf16[256,512]{1,0:T(8,128)(2,1)S(1)}, bf16[256,512]{1,0:T(8,128)(2,1)S(1)}, u32[]{:S(2)}, u32[]{:S(2)}) collective-permute-start(bf16[256,512]{1,0:T(8,128)(2,1)S(1)} %get-tuple-element.49.refs_1_), channel_id=1, source_target_pairs={{0,64},{64,128},{128,192},{192,256},{256,320},{320,384},{384,448},... | collective-permute-start | bytes 786440 | tf_op jit(solution)/shard_map/ppermute | solution.py:169
  70.7 13.0 %collective-permute-start.1 = (bf16[256,512]{1,0:T(8,128)(2,1)S(1)}, bf16[256,512]{1,0:T(8,128)(2,1)S(1)}, u32[]{:S(2)}, u32[]{:S(2)}) collective-permute-start(bf16[256,512]{1,0:T(8,128)(2,1)S(1)} %collective-permute-done.refs_4_), channel_id=1, source_target_pairs={{0,64},{64,128},{128,192},{192,256},{256,320},{320,384},{384,448},... | collective-permute-start | bytes 786440 | tf_op jit(solution)/shard_map/ppermute | solution.py:169
  72.6 13.0 %collective-permute-start.5 = (bf16[256,512]{1,0:T(8,128)(2,1)S(1)}, bf16[256,512]{1,0:T(8,128)(2,1)S(1)}, u32[]{:S(2)}, u32[]{:S(2)}) collective-permute-start(bf16[256,512]{1,0:T(8,128)(2,1)S(1)} %collective-permute-done.4.refs_3_), channel_id=1, source_target_pairs={{0,448},{64,0},{128,64},{192,128},{256,192},{320,256},{384,320},{4... | collective-permute-start | bytes 786440 | tf_op jit(solution)/shard_map/ppermute | solution.py:169
  77.8 13.0 %collective-permute-start.10 = (bf16[256,512]{1,0:T(8,128)(2,1)S(1)}, bf16[256,512]{1,0:T(8,128)(2,1)S(1)}, u32[]{:S(2)}, u32[]{:S(2)}) collective-permute-start(bf16[256,512]{1,0:T(8,128)(2,1)S(1)} %collective-permute-done.8.refs_2_), channel_id=1, source_target_pairs={{0,448},{64,0},{128,64},{192,128},{256,192},{320,256},{384,320},{4... | collective-permute-start | bytes 786440 | tf_op jit(solution)/shard_map/ppermute | solution.py:169
  80.3 13.0 %collective-permute-start.11 = (bf16[256,512]{1,0:T(8,128)(2,1)S(1)}, bf16[256,512]{1,0:T(8,128)(2,1)S(1)}, u32[]{:S(2)}, u32[]{:S(2)}) collective-permute-start(bf16[256,512]{1,0:T(8,128)(2,1)S(1)} %collective-permute-done.9.refs_5_), channel_id=1, source_target_pairs={{0,64},{64,128},{128,192},{192,256},{256,320},{320,384},{384,448},... | collective-permute-start | bytes 786440 | tf_op jit(solution)/shard_map/ppermute | solution.py:169
  83.7 13.0 %collective-permute-start.2 = (bf16[256,512]{1,0:T(8,128)(2,1)S(1)}, bf16[256,512]{1,0:T(8,128)(2,1)S(1)}, u32[]{:S(2)}, u32[]{:S(2)}) collective-permute-start(bf16[256,512]{1,0:T(8,128)(2,1)S(1)} %collective-permute-done.1.refs_8_), channel_id=1, source_target_pairs={{0,64},{64,128},{128,192},{192,256},{256,320},{320,384},{384,448},... | collective-permute-start | bytes 786440 | tf_op jit(solution)/shard_map/ppermute | solution.py:169
  85.6 13.0 %collective-permute-start.6 = (bf16[256,512]{1,0:T(8,128)(2,1)S(1)}, bf16[256,512]{1,0:T(8,128)(2,1)S(1)}, u32[]{:S(2)}, u32[]{:S(2)}) collective-permute-start(bf16[256,512]{1,0:T(8,128)(2,1)S(1)} %collective-permute-done.5.refs_7_), channel_id=1, source_target_pairs={{0,448},{64,0},{128,64},{192,128},{256,192},{320,256},{384,320},{4... | collective-permute-start | bytes 786440 | tf_op jit(solution)/shard_map/ppermute | solution.py:169
  90.8 13.0 %collective-permute-start.12 = (bf16[256,512]{1,0:T(8,128)(2,1)S(1)}, bf16[256,512]{1,0:T(8,128)(2,1)S(1)}, u32[]{:S(2)}, u32[]{:S(2)}) collective-permute-start(bf16[256,512]{1,0:T(8,128)(2,1)S(1)} %collective-permute-done.10.refs_6_), channel_id=1, source_target_pairs={{0,448},{64,0},{128,64},{192,128},{256,192},{320,256},{384,320},{4... | collective-permute-start | bytes 786440 | tf_op jit(solution)/shard_map/ppermute | solution.py:169
  93.3 10.4 %collective-permute-start.13 = (bf16[256,512]{1,0:T(8,128)(2,1)S(1)}, bf16[256,512]{1,0:T(8,128)(2,1)S(1)}, u32[]{:S(2)}, u32[]{:S(2)}) collective-permute-start(bf16[256,512]{1,0:T(8,128)(2,1)S(1)} %collective-permute-done.11.refs_9_), channel_id=1, source_target_pairs={{0,64},{64,128},{128,192},{192,256},{256,320},{320,384},{384,448},... | collective-permute-start | bytes 786440 | tf_op jit(solution)/shard_map/ppermute | solution.py:169
  96.6 9.9 %collective-permute-start.3 = (bf16[256,512]{1,0:T(8,128)(2,1)S(1)}, bf16[256,512]{1,0:T(8,128)(2,1)S(1)}, u32[]{:S(2)}, u32[]{:S(2)}) collective-permute-start(bf16[256,512]{1,0:T(8,128)(2,1)S(1)} %collective-permute-done.2.refs_12_), channel_id=1, source_target_pairs={{0,64},{64,128},{128,192},{192,256},{256,320},{320,384},{384,448},... | collective-permute-start | bytes 786440 | tf_op jit(solution)/shard_map/ppermute | solution.py:169
  98.6 9.0 %collective-permute-start.7 = (bf16[256,512]{1,0:T(8,128)(2,1)S(1)}, bf16[256,512]{1,0:T(8,128)(2,1)S(1)}, u32[]{:S(2)}, u32[]{:S(2)}) collective-permute-start(bf16[256,512]{1,0:T(8,128)(2,1)S(1)} %collective-permute-done.6.refs_11_), channel_id=1, source_target_pairs={{0,448},{64,0},{128,64},{192,128},{256,192},{320,256},{384,320},{4... | collective-permute-start | bytes 786440 | tf_op jit(solution)/shard_map/ppermute | solution.py:169
  110.2 0.9 copy-start.9
  110.2 97.8 %all-gather.6.cloned.1.call-start = ((), (), s32[]{:S(2)}) async-start(), calls=%async_computation.7 | async-start | bytes 1179648 | tf_op jit(solution)/shard_map/all_gather | solution.py:273
Sparse Core Ops, SparseCore 0:
  11.4 88.2 all-gather.3
  110.4 54.0 reduce-scatter.1
  166.5 40.9 all-gather.5
